TPU v7x, 32 devices: a whole 2x2x4 slice. The times are simulated.
32 devices in a mesh: blk: 8 (over y, x, core), exp: 4 (over z).
Axes of the slice: x: 2, y: 2, z: 4, core: 2. Of those that a mesh axis runs over, the one named last changes fastest.
Arguments:
- hidden: bfloat16 [1024, 2560], P('exp', 'blk'), may hold values from -6 to 6
- attn_gain: float32 [2560], replicated, may hold values from 0.25 to 1.75
- qkv_weight: bfloat16 [2560, 3584], P(None, 'blk'), may hold values from -0.125 to 0.125
- out_weight: bfloat16 [2560, 2560], P(None, 'blk'), may hold values from -0.125 to 0.125
- kv_pool: bfloat16 [4, 32, 128, 1024], P('exp', 'blk'), may hold values from -64 to 64
- page_table: int32 [4, 32], P('exp'), may hold values from 0 to 31, each once within a row
- cache_lens: int32 [4], P('exp'), may hold values from 1 to 3840, as said below
- ffn_gain: float32 [2560], replicated, may hold values from 0.25 to 1.75
- route_ids: int32 [1024, 6], P('exp'), may hold values from 0 to 7, all different within a row; in each aligned block of 256 rows (0 to 255, 256 to 511, ...) at most 256 rows name the same one
- route_weights: float32 [1024, 6], P('exp'), may hold values from 0.05 to 2
- shared_gate_up: bfloat16 [2560, 2, 3072], P(None, None, 'blk'), may hold values from -0.125 to 0.125
- shared_down: bfloat16 [3072, 2560], P('blk'), may hold values from -0.109375 to 0.109375
- expert_gate_up: bfloat16 [32, 2560, 768], P(('blk', 'exp')), may hold values from -0.125 to 0.125
- expert_down: bfloat16 [32, 384, 2560], P(('blk', 'exp')), may hold values from -0.3125 to 0.3125
Outputs:
- hidden_out: bfloat16 [1024, 2560], P('exp', 'blk')
- kv_pool_out: bfloat16 [4, 32, 128, 1024], P('exp', 'blk')
Inputs may be any that keep to these rules, and one draw needn't show every extreme that they name: `route_ids`: among the 256 tokens of one request at most 256 choose any one expert, and some expert is chosen by exactly 256 of them; a token's 6 experts differ. `page_table`: each row names every page of the request's pool once. `cache_lens`: some request has exactly 3840 cached tokens.
All inputs are finite; a program needn't handle non-finite values.
Results may differ from a plain program's by a relative error of at most 0.02.
The roundings to bfloat16 on the way count: a program that leaves them out, or rounds other values in their place, can miss the bound.
Values may be sent and summed in bfloat16 or wider, within the bound.
A program may use at most 256 MiB of HBM per device.

v0:
```python
import math

import jax
import jax.numpy as jnp
from jax import lax
from jax.sharding import PartitionSpec as P

HEADS = 20
KV_HEADS = 4
HEAD_DIM = 128
TOPK = 6
SPLIT = 4
PAGE = 128
NEW = 256
FF_PART = 384


rope_base = 500000.0
norm_eps = 1e-05


def normalize(inputs, gain_vec):
    values = inputs.astype(jnp.float32)
    inv_rms = lax.rsqrt(jnp.mean(values * values, axis=-1, keepdims=True) + norm_eps)
    return (values * inv_rms * gain_vec).astype(jnp.bfloat16)


def rotate(inputs, positions):
    half_dim = HEAD_DIM // 2
    frequency = rope_base ** (-(jnp.arange(half_dim).astype(jnp.float32) * 2.0 / HEAD_DIM))
    angles = positions.astype(jnp.float32)[:, None] * frequency[None, :]
    cosine = jnp.cos(angles)[:, None, :]
    sine_vals = jnp.sin(angles)[:, None, :]
    lower_half = inputs[..., :half_dim]
    upper_half = inputs[..., half_dim:]
    return jnp.concatenate(
        [
            lower_half * cosine - upper_half * sine_vals,
            upper_half * cosine + lower_half * sine_vals,
        ],
        axis=-1,
    )


def partial_softmax(queries, query_pos, block_rows, key_pos):
    key_width = KV_HEADS * HEAD_DIM
    key_rows = block_rows[:, :key_width].reshape(-1, KV_HEADS, HEAD_DIM)
    value_rows = block_rows[:, key_width:].reshape(-1, KV_HEADS, HEAD_DIM)
    scores = jnp.einsum("tkgd,skd->tkgs", queries, key_rows, preferred_element_type=jnp.float32) * (
        1.0 / math.sqrt(HEAD_DIM)
    )
    allowed = (key_pos[None, :] <= query_pos[:, None])[:, None, None, :]
    maxima = jnp.max(jnp.where(allowed, scores, -1e30), axis=-1)
    weights = jnp.where(allowed, jnp.exp(scores - maxima[..., None]), 0.0)
    totals = jnp.sum(weights, axis=-1)
    weighted = jnp.einsum(
        "tkgs,skd->tkgd",
        weights.astype(jnp.bfloat16),
        value_rows,
        preferred_element_type=jnp.float32,
    )
    return (maxima, totals, weighted)


def combine_parts(earlier, later):
    peak_early, sum_early, acc_early = earlier
    peak_late, sum_late, acc_late = later
    peak_both = jnp.maximum(peak_early, peak_late)
    factor_late = jnp.exp(peak_late - peak_both)
    return (peak_both, sum_late * factor_late, acc_late * factor_late[..., None])


def per_device(
    hidden,
    attn_gain,
    qkv_weight,
    out_weight,
    kv_pool,
    page_table,
    cache_lens,
    ffn_gain,
    route_ids,
    route_weights,
    shared_gate_up,
    shared_down,
    expert_gate_up,
    expert_down,
):
    blocks = lax.axis_size("blk")
    groups = lax.axis_size("exp")
    block_index = lax.axis_index("blk")
    model_width = hidden.shape[1] * blocks
    query_width = HEADS * HEAD_DIM
    key_width = KV_HEADS * HEAD_DIM
    group_size = HEADS // KV_HEADS
    own_rows = NEW // blocks
    full_rows = lax.all_gather(hidden, "blk", axis=1, tiled=True)
    attn_in = normalize(full_rows, attn_gain)
    projected = jnp.dot(attn_in, qkv_weight, preferred_element_type=jnp.float32).astype(
        jnp.bfloat16
    )
    projected_all = lax.all_gather(projected, "blk", axis=1, tiled=True)
    length = cache_lens[0]
    positions = length + jnp.arange(NEW, dtype=jnp.int32)
    queries = rotate(
        projected_all[:, :query_width].astype(jnp.float32).reshape(NEW, HEADS, HEAD_DIM), positions
    ).astype(jnp.bfloat16)
    fresh_keys = rotate(
        projected_all[:, query_width : query_width + key_width]
        .astype(jnp.float32)
        .reshape(NEW, KV_HEADS, HEAD_DIM),
        positions,
    ).astype(jnp.bfloat16)
    appended = jnp.concatenate(
        [fresh_keys.reshape(NEW, key_width), projected_all[:, query_width + key_width :]], axis=1
    )
    page_map = page_table[0]
    pool_pages = page_map.shape[0]
    page_index = jnp.arange(pool_pages, dtype=jnp.int32)
    logical = jnp.sum(
        jnp.where(page_map[None, :] == page_index[:, None], page_index[None, :], 0), axis=1
    )
    local_pages = kv_pool.shape[1]
    local_logical = lax.dynamic_slice_in_dim(logical, block_index * local_pages, local_pages)
    slot_offsets = jnp.arange(PAGE, dtype=jnp.int32)
    local_pos = local_logical[:, None] * PAGE + slot_offsets[None, :]
    offset = local_pos - length
    written = (offset >= 0) & (offset < NEW)
    picked = appended[jnp.clip(offset, 0, NEW - 1)]
    pool_out = jnp.where(written[:, :, None], picked, kv_pool[0])
    grouped = queries.reshape(NEW, KV_HEADS, group_size, HEAD_DIM)
    own_queries = lax.dynamic_slice_in_dim(grouped, block_index * own_rows, own_rows, 0)
    own_pos = lax.dynamic_slice_in_dim(positions, block_index * own_rows, own_rows, 0)
    initial = (
        jnp.full((own_rows, KV_HEADS, group_size), -1e30, jnp.float32),
        jnp.zeros((own_rows, KV_HEADS, group_size), jnp.float32),
        jnp.zeros((own_rows, KV_HEADS, group_size, HEAD_DIM), jnp.float32),
    )
    shard_pages = lax.all_gather(pool_out, "blk", axis=0, tiled=True)
    page_count = shard_pages.shape[0]
    key_pos = (logical[:, None] * PAGE + slot_offsets[None, :]).reshape(-1)
    block_rows = shard_pages.reshape(page_count * PAGE, 2 * key_width)
    maxima, totals, weighted = combine_parts(
        initial, partial_softmax(own_queries, own_pos, block_rows, key_pos)
    )
    own_attention = (
        (weighted / totals[..., None]).reshape(own_rows, query_width).astype(jnp.bfloat16)
    )
    attended = jnp.dot(
        lax.all_gather(own_attention, "blk", axis=0, tiled=True),
        out_weight,
        preferred_element_type=jnp.float32,
    )
    mixed_cols = (hidden.astype(jnp.float32) + attended).astype(jnp.bfloat16)
    mixed_rows = lax.all_gather(mixed_cols, "blk", axis=1, tiled=True)
    ffn_in = normalize(mixed_rows, ffn_gain)
    shared_cols = shared_gate_up.shape[2]
    gate_up = jnp.dot(
        ffn_in,
        shared_gate_up.reshape(model_width, 2 * shared_cols),
        preferred_element_type=jnp.float32,
    )
    shared_act = (jax.nn.silu(gate_up[:, :shared_cols]) * gate_up[:, shared_cols:]).astype(
        jnp.bfloat16
    )
    shared_term = jnp.dot(shared_act, shared_down, preferred_element_type=jnp.float32)
    row_experts = groups // SPLIT
    expert_count = row_experts * blocks
    capacity = NEW * TOPK * 4 // (expert_count * 3)
    row_expert_ids = block_index * row_experts + jnp.arange(row_experts, dtype=jnp.int32)
    route_hits = route_ids[:, :, None] == row_expert_ids[None, None, :]
    chosen = jnp.any(route_hits, axis=1)
    route_share = jnp.sum(jnp.where(route_hits, route_weights[:, :, None], 0.0), axis=1)
    slot_rank = jnp.cumsum(chosen.astype(jnp.int32), axis=0) - 1
    slot_ids = jnp.arange(capacity, dtype=jnp.int32)
    placed = chosen.T[:, None, :] & (slot_rank.T[:, None, :] == slot_ids[None, :, None])
    selector = placed.astype(jnp.bfloat16)
    outgoing = jnp.einsum(
        "ect,td->ecd", selector, ffn_in, preferred_element_type=jnp.float32
    ).astype(jnp.bfloat16)
    outgoing = jnp.repeat(outgoing, SPLIT, axis=0)
    received = lax.all_to_all(outgoing, "exp", split_axis=0, concat_axis=0, tiled=True)
    flat_rows = received.reshape(-1, model_width)
    expert_gu = jnp.dot(flat_rows, expert_gate_up[0], preferred_element_type=jnp.float32)
    activated = (jax.nn.silu(expert_gu[:, :FF_PART]) * expert_gu[:, FF_PART:]).astype(jnp.bfloat16)
    result = jnp.dot(activated, expert_down[0], preferred_element_type=jnp.float32).astype(
        jnp.bfloat16
    )
    returned = lax.all_to_all(
        result.reshape(received.shape), "exp", split_axis=0, concat_axis=0, tiled=True
    )
    summed = jnp.sum(
        returned.reshape(row_experts, SPLIT, capacity, model_width).astype(jnp.float32), axis=1
    )
    slot_weight = jnp.sum(placed.astype(jnp.float32) * route_share.T[:, None, :], axis=2)
    slot_values = summed * slot_weight[:, :, None]
    upper_part = slot_values.astype(jnp.bfloat16)
    lower_part = (slot_values - upper_part.astype(jnp.float32)).astype(jnp.bfloat16)
    routed = jnp.einsum(
        "ect,ecd->td", selector, upper_part, preferred_element_type=jnp.float32
    ) + jnp.einsum("ect,ecd->td", selector, lower_part, preferred_element_type=jnp.float32)
    layer_term = shared_term + routed
    summed_cols = lax.psum_scatter(layer_term, "blk", scatter_dimension=1, tiled=True)
    hidden_out = (mixed_cols.astype(jnp.float32) + summed_cols).astype(jnp.bfloat16)
    return (hidden_out, pool_out[None])


def solution(mesh):
    placed = (
        P("exp", "blk"),
        P(),
        P(None, "blk"),
        P(None, "blk"),
        P("exp", "blk", None, None),
        P("exp", None),
        P("exp"),
        P(),
        P("exp", None),
        P("exp", None),
        P(None, None, "blk"),
        P("blk", None),
        P(("blk", "exp"), None, None),
        P(("blk", "exp"), None, None),
    )
    return jax.shard_map(
        per_device,
        mesh=mesh,
        in_specs=placed,
        out_specs=(P("exp", "blk"), P("exp", "blk", None, None)),
        check_vma=False,
    )
```

profile of v0, /device:TPU:0, one launch (start us, length us, event | category | flops | bytes accessed | tf_op | source)
XLA Modules:
  0.0 528.2 jit_solution(4073500380773647609)
XLA Ops:
  8.0 29.3 %all-gather.6.cloned.1.call-done = bf16[256,2560]{0,1:T(8,128)(2,1)} async-done(((bf16[256,320]{0,1:T(8,128)(2,1)}), bf16[256,2560]{0,1:T(8,128)(2,1)}) %all-gather.6.cloned.1.call-update) | async-done | bytes 1310736 | tf_op jit(solution)/shard_map/all_gather | solution.py:97
  38.9 2.9 fusion.29
  43.2 25.6 %all-gather.8.cloned.1.call-done = bf16[256,3584]{0,1:T(8,128)(2,1)} async-done(((bf16[256,448]{0,1:T(8,128)(2,1)}), bf16[256,3584]{0,1:T(8,128)(2,1)}) %all-gather.8.cloned.1.call-update) | async-done | bytes 1835024 | tf_op jit(solution)/shard_map/all_gather | solution.py:102
  79.6 48.5 %all-gather.10.cloned.1.call-done = bf16[32,128,1024]{2,1,0:T(8,128)(2,1)} async-done(((bf16[4,128,1024]{2,1,0:T(8,128)(2,1)}), bf16[32,128,1024]{2,1,0:T(8,128)(2,1)}) %all-gather.10.cloned.1.call-update) | async-done | bytes 8388624 | tf_op jit(solution)/shard_map/all_gather | solution.py:139
  128.1 6.0 %fusion.82 = (bf16[4096,512]{1,0:T(8,128)(2,1)}, bf16[4096,512]{1,0:T(8,128)(2,1)}) fusion(bf16[4096,1024]{1,0:T(8,128)(2,1)} %bitcast.93), kind=kLoop, calls=%fused_computation.114 | loop fusion | bytes 16777216 | tf_op jit(solution)/shard_map/slice | solution.py:47
  134.0 6.4 %copy.48 = bf16[4096,512]{0,1:T(8,128)(2,1)} copy(bf16[4096,512]{1,0:T(8,128)(2,1)} %get-tuple-element.4) | data formatting | bytes 8388608
  140.5 4.1 fusion
  144.6 2.6 fusion.3
  148.5 6.5 %copy.47 = bf16[4096,512]{0,1:T(8,128)(2,1)} copy(bf16[4096,512]{1,0:T(8,128)(2,1)} %get-tuple-element.5) | data formatting | bytes 8388608
  155.0 7.3 %fusion.42 = bf16[32,4,5,128]{3,0,2,1:T(8,128)(2,1)S(1)} fusion(bf16[4096,4,128,1]{0,2,3,1:T(8,128)(2,1)} %bitcast.99, f32[4,4096,32,5]{1,2,3,0:T(8,128)} %copy-done.2, f32[32,4,5]{0,2,1:T(8,128)S(1)} %get-tuple-element.16, pred[32,4096]{1,0:T(8,128)(4,1)S(1)} %broadcast_compare_fusion, f32[32,4,5]{0,2,1:T(8,128)S(1)} %get-tuple-element.13, ...), kind=kOutput, calls=%fused_computation.51 | convolution fusion | flops 681820160 | bytes 14982656 | tf_op jit(solution)/shard_map/tkgs,skd->tkgd/dot_general | solution.py:56
  163.5 24.5 %all-gather.12.cloned.1.call-done = bf16[256,2560]{1,0:T(8,128)(2,1)} async-done(((bf16[32,2560]{1,0:T(8,128)(2,1)}), bf16[256,2560]{1,0:T(8,128)(2,1)}) %all-gather.12.cloned.1.call-update) | async-done | bytes 1310736 | tf_op jit(solution)/shard_map/all_gather | solution.py:150
  188.0 3.1 fusion.38
  192.0 23.9 %all-gather.14.cloned.1.call-done = bf16[256,2560]{0,1:T(8,128)(2,1)} async-done(((bf16[256,320]{0,1:T(8,128)(2,1)}), bf16[256,2560]{0,1:T(8,128)(2,1)}) %all-gather.14.cloned.1.call-update) | async-done | bytes 1310736 | tf_op jit(solution)/shard_map/all_gather | solution.py:155
  220.0 120.7 %all_to_all.10 = bf16[4,256,2560]{2,1,0:T(8,128)(2,1)S(1)} all-to-all(bf16[4,256,2560]{2,1,0:T(8,128)(2,1)S(1)} %reshape.513), channel_id=1, replica_groups=mesh['blk'=8,'exp'=4] {'exp'}, dimensions={0} | all-to-all | bytes 10485760 | tf_op jit(solution)/shard_map/all_to_all | solution.py:182
  340.7 4.2 fusion.12
  344.9 4.7 convolution_convert_fusion
  349.6 5.1 all-to-all-start.1
  355.0 2.9 copy.49
  359.6 2.5 fusion.56
  362.1 107.9 %all-to-all-done.1 = bf16[4,256,2560]{2,1,0:T(8,128)(2,1)} async-done(((bf16[4,256,2560]{2,1,0:T(8,128)(2,1)}), bf16[4,256,2560]{2,1,0:T(8,128)(2,1)}, u32[]{:S(2)}, u32[]{:S(2)}) %all-to-all-start.1) | async-done | bytes 5242912 | tf_op jit(solution)/shard_map/all_to_all | solution.py:189
  470.0 3.6 convert_reduce_fusion
  475.4 2.4 fusion.11
  477.8 2.6 broadcast_select_fusion
  480.3 39.4 %reduce-scatter.2.cloned.1.call-done = f32[256,320]{0,1:T(8,128)} async-done(((f32[256,2560]{0,1:T(8,128)}), f32[256,320]{0,1:T(8,128)}) %reduce-scatter.2.cloned.1.call-update) | async-done | bytes 327696 | tf_op jit(solution)/shard_map/reduce_scatter | solution.py:203
  (91 shorter events, 26.7 us)
Async XLA Ops:
  7.2 31.8 %copy-start = (bf16[2560,448]{0,1:T(8,128)(2,1)S(1)}, bf16[2560,448]{0,1:T(8,128)(2,1)}, u32[]{:S(2)}) copy-start(bf16[2560,448]{0,1:T(8,128)(2,1)} %param.16) | copy-start | bytes 6881284
  7.2 30.1 %all-gather.6.cloned.1.call-start = ((), (), s32[]{:S(2)}) async-start(), calls=%async_computation.3 | async-start | bytes 1474560 | tf_op jit(solution)/shard_map/all_gather | solution.py:97
  7.9 60.9 %all-gather.8.cloned.1.call-start = ((), (), s32[]{:S(2)}) async-start(), calls=%async_computation.4 | async-start | bytes 2064384 | tf_op jit(solution)/shard_map/all_gather | solution.py:102
  38.9 3.6 copy-start.14
  41.9 86.2 %all-gather.10.cloned.1.call-start = ((), (), s32[]{:S(2)}) async-start(), calls=%async_computation.5 | async-start | bytes 9437184 | tf_op jit(solution)/shard_map/all_gather | solution.py:139
  70.3 2.1 copy-start.4
  73.5 1.3 slice-start
  73.5 114.5 %all-gather.12.cloned.1.call-start = ((), (), s32[]{:S(2)}) async-start(), calls=%async_computation.6 | async-start | bytes 1474560 | tf_op jit(solution)/shard_map/all_gather | solution.py:150
  144.5 4.0 copy-start.2
  155.0 33.0 %copy-start.8 = (bf16[256,320]{0,1:T(8,128)(2,1)S(1)}, bf16[256,320]{0,1:T(8,128)(2,1)}, u32[]{:S(2)}) copy-start(bf16[256,320]{0,1:T(8,128)(2,1)} %param.14) | copy-start | bytes 491524
  162.3 28.9 %copy-start.9 = (f32[256,6]{0,1:T(8,128)S(1)}, f32[256,6]{0,1:T(8,128)}, u32[]{:S(2)}) copy-start(f32[256,6]{0,1:T(8,128)} %param.23) | copy-start | bytes 18436
  162.3 28.9 %copy-start.10 = (s32[256,6]{0,1:T(8,128)S(1)}, s32[256,6]{0,1:T(8,128)}, u32[]{:S(2)}) copy-start(s32[256,6]{0,1:T(8,128)} %param.22) | copy-start | bytes 18436
  163.3 54.4 %copy-start.13 = (f32[2560]{0:T(1024)S(1)}, f32[2560]{0:T(1024)}, u32[]{:S(2)}) copy-start(f32[2560]{0:T(1024)} %param.21) | copy-start | bytes 30724
  163.3 52.7 %all-gather.14.cloned.1.call-start = ((), (), s32[]{:S(2)}) async-start(), calls=%async_computation.7 | async-start | bytes 1474560 | tf_op jit(solution)/shard_map/all_gather | solution.py:155
  220.0 120.7 %copy-start.11 = (bf16[1,2560,768]{2,1,0:T(8,128)(2,1)S(1)}, bf16[1,2560,768]{2,1,0:T(8,128)(2,1)}, u32[]{:S(2)}) copy-start(bf16[1,2560,768]{2,1,0:T(8,128)(2,1)} %param.26) | copy-start | bytes 11796484
  340.7 4.2 copy-start.12
  349.6 120.3 %all-to-all-start.1 = ((bf16[4,256,2560]{2,1,0:T(8,128)(2,1)}), bf16[4,256,2560]{2,1,0:T(8,128)(2,1)}, u32[]{:S(2)}, u32[]{:S(2)}) async-start(bf16[4,256,2560]{2,1,0:T(8,128)(2,1)} %bitcast.96), calls=%async_computation.1 | async-start | bytes 10485760 | tf_op jit(solution)/shard_map/all_to_all | solution.py:189
  354.7 165.0 %reduce-scatter.2.cloned.1.call-start = ((), (), s32[]{:S(2)}) async-start(), calls=%async_computation.8 | async-start | bytes 2949120 | tf_op jit(solution)/shard_map/reduce_scatter | solution.py:203
  355.0 3.0 copy-start.6
  358.0 1.5 copy-start.5
  473.6 1.7 copy-start.3
  477.7 43.6 %copy-start.1 = (bf16[2560,448]{0,1:T(8,128)(2,1)S(1)}, bf16[2560,448]{0,1:T(8,128)(2,1)}, u32[]{:S(2)}) copy-start(bf16[2560,448]{0,1:T(8,128)(2,1)} %param.16) | copy-start | bytes 6881284
  477.7 42.0 %copy-start.7 = (bf16[256,320]{0,1:T(8,128)(2,1)S(1)}, bf16[256,320]{0,1:T(8,128)(2,1)}, u32[]{:S(2)}) copy-start(bf16[256,320]{0,1:T(8,128)(2,1)} %fusion.38) | copy-start | bytes 491524
Sparse Core Ops, SparseCore 0:
  9.9 27.2 all-gather.5
  42.0 26.7 all-gather.7
  73.7 54.3 all-gather.9
  163.4 24.5 all-gather.11
  191.3 24.5 all-gather.13
  477.9 41.7 reduce-scatter.1
where the time goes:
time: 529 us; the launch traced here: 528 us
  waiting for transfers between devices  300 us (57%)
  blocking collectives  121 us (23%)
  matrix products  35.3 us (7%)
  local copies, waits for them, and re-layouts  33.3 us (6%)
  other arithmetic  18.3 us (3%)
  between operations  15.1 us (3%)
  starting transfers between devices  5.7 us (1%)
    all_to_all x1, blocking collectives, per_device(): lax.all_to_all(outgoing, 'exp', split_axis=0, concat_axis=0, tiled=True)  121 us
    all_to_all x1, waiting for transfers between devices, per_device(): lax.all_to_all(result.reshape(received.shape), 'exp', split_axis=0, conca...  108 us
    all_gather x1, waiting for transfers between devices, per_device(): shard_pages = lax.all_gather(pool_out, 'blk', axis=0, tiled=True)  48.5 us
    reduce_scatter x1, waiting for transfers between devices, per_device(): lax.psum_scatter(layer_term, 'blk', scatter_dimension=1, tiled=True)  39.4 us
    all_gather x1, waiting for transfers between devices, per_device(): full_rows = lax.all_gather(hidden, 'blk', axis=1, tiled=True)  29.3 us
    all_gather x1, waiting for transfers between devices, per_device(): projected_all = lax.all_gather(projected, 'blk', axis=1, tiled=True)  25.6 us
    all_gather x1, waiting for transfers between devices, per_device(): lax.all_gather(own_attention, 'blk', axis=0, tiled=True)  24.5 us
    all_gather x1, waiting for transfers between devices, per_device(): mixed_rows = lax.all_gather(mixed_cols, 'blk', axis=1, tiled=True)  23.9 us
  transfers between devices with their start and end apart: 7, of which 7 were waited for; matrix products, arithmetic and copies ran while one was open for 3% of the time, Pallas kernels for 0%

commit v1 on v0

v1 whole, which is shorter than its diff:
```python
import functools
import math

import jax
import jax.numpy as jnp
from jax import lax
from jax.experimental import pallas as pl
from jax.experimental.pallas import tpu as pltpu
from jax.sharding import PartitionSpec as P

HEADS = 20
KV_HEADS = 4
HEAD_DIM = 128
TOPK = 6
SPLIT = 4
PAGE = 128
NEW = 256
FF_PART = 384
GROUP = HEADS // KV_HEADS

MESH = pl.DeviceIdType.MESH
VM = pltpu.VMEM
F32 = jnp.float32
BF16 = jnp.bfloat16

rope_base = 500000.0
norm_eps = 1e-05


def remote(src, dst, send, recv, **to):
    return pltpu.make_async_remote_copy(
        src_ref=src, dst_ref=dst, send_sem=send, recv_sem=recv, device_id=to, device_id_type=MESH
    )


def greet(peers):
    barrier = pltpu.get_barrier_semaphore()
    for to in peers:
        pl.semaphore_signal(barrier, inc=1, device_id=to, device_id_type=MESH)
    pl.semaphore_wait(barrier, len(peers))


def place(half):
    me = lax.axis_index("blk")
    chip, core = me // 2, me % 2
    partner = chip * 2 + 1 - core

    def peer(k):
        return ((chip + k + half) % half) * 2 + core

    return me, partner, peer


def gather_kernel(n, x_ref, o_ref, local_sem, send, recv, fsend, frecv):
    half = n // 2
    me, partner, peer = place(half)
    rows = x_ref.shape[0]

    def block(b):
        return o_ref.at[pl.ds(pl.multiple_of(b * rows, 8), rows), :]

    greet([{"blk": peer(k)} for k in range(1, half)] + [{"blk": partner}])
    outs = [remote(x_ref, block(me), send.at[k], recv.at[k], blk=peer(k)) for k in range(1, half)]
    for copy in outs:
        copy.start()
    passed = [remote(x_ref, block(me), fsend.at[0], frecv.at[0], blk=partner)]
    passed[0].start()
    own = pltpu.make_async_copy(x_ref, block(me), local_sem)
    own.start()
    for k in range(1, half):
        outs[k - 1].wait_recv()
        b = peer(-k)
        copy = remote(block(b), block(b), fsend.at[k], frecv.at[k], blk=partner)
        copy.start()
        passed.append(copy)
    for copy in outs:
        copy.wait_send()
    for copy in passed:
        copy.wait()
    own.wait()


def gather_blk(x, collective_id):
    n = lax.axis_size("blk")
    half = n // 2
    dma = pltpu.SemaphoreType.DMA
    return pl.pallas_call(
        functools.partial(gather_kernel, n),
        out_shape=jax.ShapeDtypeStruct((n * x.shape[0], x.shape[1]), x.dtype),
        in_specs=[pl.BlockSpec(memory_space=VM)],
        out_specs=pl.BlockSpec(memory_space=VM),
        scratch_shapes=[dma] + [dma((half,))] * 4,
        compiler_params=pltpu.CompilerParams(
            collective_id=collective_id, has_side_effects=True, vmem_limit_bytes=32 << 20
        ),
        name="gather_blk%d" % collective_id,
    )(x)


def reduce_kernel(n, x_ref, o_ref, r1, s, r2, send1, recv1, send2, recv2):
    half = n // 2
    me, partner, peer = place(half)
    rows = o_ref.shape[0]

    def block(b):
        return pl.ds(pl.multiple_of(b * rows, 16), rows)

    greet([{"blk": peer(k)} for k in range(1, half)] + [{"blk": partner}])
    order = list(range(1, half)) + [0]
    first = {}
    for k in order:
        other = peer(k) + partner - me
        first[k] = remote(x_ref.at[block(other), :], r1.at[k], send1.at[k], recv1.at[k], blk=partner)
        first[k].start()
    second = []
    for k in order:
        first[k].wait_recv()
        s[k] = (x_ref[block(peer(k)), :].astype(F32) + r1[k].astype(F32)).astype(BF16)
        if k:
            copy = remote(s.at[k], r2.at[k], send2.at[k], recv2.at[k], blk=peer(k))
            copy.start()
            second.append(copy)
    total = x_ref[block(me), :].astype(F32) + r1[0].astype(F32)
    for k in range(1, half):
        second[k - 1].wait_recv()
        total += r2[k].astype(F32)
    o_ref[...] = total.astype(o_ref.dtype)
    for k in order:
        first[k].wait_send()
    for copy in second:
        copy.wait_send()


def reduce_blk(x, collective_id):
    n = lax.axis_size("blk")
    half = n // 2
    dma = pltpu.SemaphoreType.DMA
    rows, cols = x.shape[0] // n, x.shape[1]
    return pl.pallas_call(
        functools.partial(reduce_kernel, n),
        out_shape=jax.ShapeDtypeStruct((rows, cols), BF16),
        in_specs=[pl.BlockSpec(memory_space=VM)],
        out_specs=pl.BlockSpec(memory_space=VM),
        scratch_shapes=[VM((half, rows, cols), BF16)] * 3 + [dma((half,))] * 4,
        compiler_params=pltpu.CompilerParams(
            collective_id=collective_id, has_side_effects=True, vmem_limit_bytes=32 << 20
        ),
        name="reduce_blk",
    )(x)


def gather_all_kernel(n, g, x_ref, o_ref, local_sem, zsend, zrecv, bsend, brecv, psend, precv):
    half = n // 2
    me, partner, peer = place(half)
    z = lax.axis_index("exp")
    rows, cols = x_ref.shape

    def zpeer(k):
        return (z + k + g) % g

    def block(b, w):
        return o_ref.at[
            pl.ds(pl.multiple_of(b * rows, 16), rows), pl.ds(pl.multiple_of(w * cols, 128), cols)
        ]

    greet(
        [{"exp": zpeer(k)} for k in range(1, g)]
        + [{"blk": peer(k)} for k in range(1, half)]
        + [{"blk": partner}]
    )
    along = [
        remote(x_ref, block(me, z), zsend.at[k], zrecv.at[k], exp=zpeer(k)) for k in range(1, g)
    ]
    for copy in along:
        copy.start()
    own = pltpu.make_async_copy(x_ref, block(me, z), local_sem)
    own.start()
    outs, passed = {}, []

    def spread(kz):
        w = zpeer(-kz)
        src = x_ref if kz == 0 else block(me, w)
        for k in range(1, half):
            outs[kz, k] = remote(src, block(me, w), bsend.at[kz, k], brecv.at[kz, k], blk=peer(k))
            outs[kz, k].start()
        copy = remote(src, block(me, w), psend.at[kz, 0], precv.at[kz, 0], blk=partner)
        copy.start()
        passed.append(copy)

    def relay(kz):
        w = zpeer(-kz)
        for k in range(1, half):
            outs[kz, k].wait_recv()
            here = block(peer(-k), w)
            copy = remote(here, here, psend.at[kz, k], precv.at[kz, k], blk=partner)
            copy.start()
            passed.append(copy)

    spread(0)
    for kz in range(1, g):
        along[kz - 1].wait_recv()
        spread(kz)
        relay(kz - 1)
    relay(g - 1)
    for copy in along + list(outs.values()):
        copy.wait_send()
    for copy in passed:
        copy.wait()
    own.wait()


def gather_all(x, collective_id):
    n, g = lax.axis_size("blk"), lax.axis_size("exp")
    half = n // 2
    if n * g > 32:
        along = lax.all_gather(x, "exp", axis=1, tiled=True)
        return lax.all_gather(along, "blk", axis=0, tiled=True)
    dma = pltpu.SemaphoreType.DMA
    return pl.pallas_call(
        functools.partial(gather_all_kernel, n, g),
        out_shape=jax.ShapeDtypeStruct((n * x.shape[0], g * x.shape[1]), x.dtype),
        in_specs=[pl.BlockSpec(memory_space=VM)],
        out_specs=pl.BlockSpec(memory_space=VM),
        scratch_shapes=[dma] + [dma((g,))] * 2 + [dma((g, half))] * 4,
        compiler_params=pltpu.CompilerParams(
            collective_id=collective_id, has_side_effects=True, vmem_limit_bytes=40 << 20
        ),
        name="gather_all",
    )(x)


def reduce_all_kernel(
    n, g, x_ref, o_ref, r1, s, r2, t, r3, send1, recv1, send2, recv2, send3, recv3
):
    half = n // 2
    me, partner, peer = place(half)
    z = lax.axis_index("exp")
    rows, cols = o_ref.shape

    def zpeer(k):
        return (z + k + g) % g

    def at(b, w):
        return (
            pl.ds(pl.multiple_of(b * rows, 16), rows),
            pl.ds(pl.multiple_of(w * cols, 128), cols),
        )

    greet(
        [{"exp": zpeer(k)} for k in range(1, g)]
        + [{"blk": peer(k)} for k in range(1, half)]
        + [{"blk": partner}]
    )
    chunks = list(range(1, g)) + [0]
    order = list(range(1, half)) + [0]
    first, second, third = {}, {}, {}
    for kz in chunks:
        for k in order:
            other = peer(k) + partner - me
            first[kz, k] = remote(
                x_ref.at[at(other, zpeer(kz))],
                r1.at[kz, k],
                send1.at[kz, k],
                recv1.at[kz, k],
                blk=partner,
            )
            first[kz, k].start()

    def pair(kz):
        for k in order:
            first[kz, k].wait_recv()
            if k:
                mine = x_ref[at(peer(k), zpeer(kz))].astype(F32)
                s[kz, k] = (mine + r1[kz, k].astype(F32)).astype(BF16)
                second[kz, k] = remote(
                    s.at[kz, k], r2.at[kz, k], send2.at[kz, k], recv2.at[kz, k], blk=peer(k)
                )
                second[kz, k].start()

    def finish(kz):
        total = x_ref[at(me, zpeer(kz))].astype(F32) + r1[kz, 0].astype(F32)
        for k in range(1, half):
            second[kz, k].wait_recv()
            total += r2[kz, k].astype(F32)
        if kz:
            t[kz] = total.astype(BF16)
            third[kz] = remote(t.at[kz], r3.at[kz], send3.at[kz], recv3.at[kz], exp=zpeer(kz))
            third[kz].start()
        return total

    for kz in chunks:
        pair(kz)
    for kz in chunks:
        total = finish(kz)
    for kz in range(1, g):
        third[kz].wait_recv()
        total += r3[kz].astype(F32)
    o_ref[...] = total
    for copy in list(first.values()) + list(second.values()) + list(third.values()):
        copy.wait_send()


def reduce_all(x, collective_id):
    n, g = lax.axis_size("blk"), lax.axis_size("exp")
    half = n // 2
    if n * g > 32:
        part = lax.psum_scatter(x, "blk", scatter_dimension=0, tiled=True)
        return lax.psum_scatter(part, "exp", scatter_dimension=1, tiled=True).astype(F32)
    dma = pltpu.SemaphoreType.DMA
    rows, cols = x.shape[0] // n, x.shape[1] // g
    return pl.pallas_call(
        functools.partial(reduce_all_kernel, n, g),
        out_shape=jax.ShapeDtypeStruct((rows, cols), F32),
        in_specs=[pl.BlockSpec(memory_space=VM)],
        out_specs=pl.BlockSpec(memory_space=VM),
        scratch_shapes=[VM((g, half, rows, cols), BF16)] * 3
        + [VM((g, rows, cols), BF16)] * 2
        + [dma((g, half))] * 4
        + [dma((g,))] * 2,
        compiler_params=pltpu.CompilerParams(
            collective_id=collective_id, has_side_effects=True, vmem_limit_bytes=40 << 20
        ),
        name="reduce_all",
    )(x)


def attend_kernel(q_ref, k_ref, v_ref, kpos_ref, qpos_ref, acc_ref, max_ref, sum_ref):
    allowed = kpos_ref[...] <= qpos_ref[...]
    keys, vals = k_ref[...], v_ref[...]
    for h in range(GROUP):
        scores = jnp.dot(keys, q_ref[h], preferred_element_type=F32) * (1.0 / math.sqrt(HEAD_DIM))
        scores = jnp.where(allowed, scores, -1e30)
        peak = jnp.max(scores, axis=0, keepdims=True)
        weights = jnp.where(allowed, jnp.exp(scores - peak), 0.0)
        max_ref[0, pl.ds(h, 1), :] = peak
        sum_ref[0, pl.ds(h, 1), :] = jnp.sum(weights, axis=0, keepdims=True)
        acc_ref[h] = lax.dot_general(
            vals, weights.astype(BF16), (((0,), (0,)), ((), ())), preferred_element_type=F32
        )


def attend_local(queries, rows, key_pos, query_pos):
    slots = rows.shape[0]
    stat = jax.ShapeDtypeStruct((KV_HEADS, GROUP, NEW), F32)
    return pl.pallas_call(
        attend_kernel,
        grid=(KV_HEADS,),
        out_shape=(jax.ShapeDtypeStruct((HEADS, HEAD_DIM, NEW), F32), stat, stat),
        in_specs=[
            pl.BlockSpec((GROUP, HEAD_DIM, NEW), lambda i: (i, 0, 0)),
            pl.BlockSpec((slots, HEAD_DIM), lambda i: (0, i)),
            pl.BlockSpec((slots, HEAD_DIM), lambda i: (0, i + KV_HEADS)),
            pl.BlockSpec((slots, 1), lambda i: (0, 0)),
            pl.BlockSpec((1, NEW), lambda i: (0, 0)),
        ],
        out_specs=(
            pl.BlockSpec((GROUP, HEAD_DIM, NEW), lambda i: (i, 0, 0)),
            pl.BlockSpec((1, GROUP, NEW), lambda i: (i, 0, 0)),
            pl.BlockSpec((1, GROUP, NEW), lambda i: (i, 0, 0)),
        ),
        compiler_params=pltpu.CompilerParams(vmem_limit_bytes=32 << 20),
        name="attend_local",
    )(queries, rows, rows, key_pos[:, None], query_pos[None, :])


def normalize(inputs, gain_vec):
    values = inputs.astype(F32)
    inv_rms = lax.rsqrt(jnp.mean(values * values, axis=0, keepdims=True) + norm_eps)
    return (values * inv_rms * gain_vec[:, None]).astype(BF16)


def rotate(inputs, positions):
    half_dim = HEAD_DIM // 2
    frequency = rope_base ** (-(jnp.arange(half_dim).astype(F32) * 2.0 / HEAD_DIM))
    angles = frequency[:, None] * positions.astype(F32)[None, :]
    cosine = jnp.cos(angles)[None]
    sine_vals = jnp.sin(angles)[None]
    lower_half = inputs[:, :half_dim]
    upper_half = inputs[:, half_dim:]
    return jnp.concatenate(
        [
            lower_half * cosine - upper_half * sine_vals,
            upper_half * cosine + lower_half * sine_vals,
        ],
        axis=1,
    )


def columns_dot(weight, inputs):
    return lax.dot_general(weight, inputs, (((0,), (0,)), ((), ())), preferred_element_type=F32)


def per_device(
    hidden,
    attn_gain,
    qkv_weight,
    out_weight,
    kv_pool,
    page_table,
    cache_lens,
    ffn_gain,
    route_ids,
    route_weights,
    shared_gate_up,
    shared_down,
    expert_gate_up,
    expert_down,
):
    blocks = lax.axis_size("blk")
    groups = lax.axis_size("exp")
    block_index = lax.axis_index("blk")
    group_index = lax.axis_index("exp")
    model_width = hidden.shape[1] * blocks
    query_width = HEADS * HEAD_DIM
    key_width = KV_HEADS * HEAD_DIM

    expert_count = blocks * groups // SPLIT
    experts = jnp.arange(expert_count, dtype=jnp.int32)
    hits = route_ids.T[None] == experts[:, None, None]
    shares = jnp.sum(jnp.where(hits, route_weights.T[None], 0.0), axis=1)
    all_shares = lax.all_gather(shares, "exp", axis=1, tiled=True)
    own_expert = (block_index * groups + group_index) // SPLIT
    share = lax.dynamic_slice_in_dim(all_shares, own_expert, 1, 0)

    hidden_t = hidden.T
    attn_in = normalize(gather_blk(hidden_t, 1), attn_gain)
    projected = columns_dot(qkv_weight, attn_in).astype(BF16)
    projected_all = gather_blk(projected, 2)
    length = cache_lens[0]
    positions = length + jnp.arange(NEW, dtype=jnp.int32)
    turned = rotate(
        projected_all[: query_width + key_width].astype(F32).reshape(-1, HEAD_DIM, NEW), positions
    ).astype(BF16)
    queries = turned[:HEADS]
    appended = jnp.concatenate(
        [turned[HEADS:].reshape(key_width, NEW), projected_all[query_width + key_width :]], axis=0
    ).T

    page_map = page_table[0]
    pool_pages = page_map.shape[0]
    page_index = jnp.arange(pool_pages, dtype=jnp.int32)
    logical = jnp.sum(
        jnp.where(page_map[None, :] == page_index[:, None], page_index[None, :], 0), axis=1
    )
    local_pages = kv_pool.shape[1]
    local_logical = lax.dynamic_slice_in_dim(logical, block_index * local_pages, local_pages)
    slot_offsets = jnp.arange(PAGE, dtype=jnp.int32)
    local_pos = local_logical[:, None] * PAGE + slot_offsets[None, :]
    offset = local_pos - length
    written = (offset >= 0) & (offset < NEW)
    picked = appended[jnp.clip(offset, 0, NEW - 1)]
    pool_out = jnp.where(written[:, :, None], picked, kv_pool[0])

    acc, peaks, sums = attend_local(
        queries,
        pool_out.reshape(local_pages * PAGE, 2 * key_width),
        local_pos.reshape(-1),
        positions,
    )
    stats = jnp.concatenate([peaks.reshape(HEADS, NEW), sums.reshape(HEADS, NEW)], axis=0)
    all_stats = gather_blk(stats, 3).reshape(blocks, 2, HEADS, NEW)
    top = jnp.max(all_stats[:, 0], axis=0)
    whole = jnp.sum(all_stats[:, 1] * jnp.exp(all_stats[:, 0] - top[None]), axis=0)
    factor = jnp.exp(stats[:HEADS] - top) / whole
    scaled = (acc * factor[:, None, :]).astype(BF16).reshape(query_width, NEW)
    attention = gather_blk(reduce_blk(scaled, 4), 5)
    attended = columns_dot(out_weight, attention)
    mixed = (hidden_t.astype(F32) + attended).astype(BF16)

    ffn_in = normalize(gather_all(mixed, 6), ffn_gain)
    own_in = lax.dynamic_slice_in_dim(ffn_in, group_index * NEW, NEW, 1)
    shared_cols = shared_gate_up.shape[2]
    gate_up = columns_dot(shared_gate_up.reshape(model_width, 2 * shared_cols), own_in)
    shared_act = (jax.nn.silu(gate_up[:shared_cols]) * gate_up[shared_cols:]).astype(BF16)
    shared_term = columns_dot(shared_down, shared_act)

    expert_gu = columns_dot(expert_gate_up[0], ffn_in)
    activated = (jax.nn.silu(expert_gu[:FF_PART]) * expert_gu[FF_PART:]).astype(BF16)
    result = columns_dot(expert_down[0], activated) * share
    mine = (jnp.arange(groups, dtype=jnp.int32) == group_index)[None, :, None]
    layer = result.reshape(model_width, groups, NEW) + jnp.where(mine, shared_term[:, None, :], 0.0)
    summed = reduce_all(layer.astype(BF16).reshape(model_width, groups * NEW), 7)
    hidden_out = (mixed.astype(F32) + summed).astype(BF16)
    return (hidden_out.T, pool_out[None])


def solution(mesh):
    placed = (
        P("exp", "blk"),
        P(),
        P(None, "blk"),
        P(None, "blk"),
        P("exp", "blk", None, None),
        P("exp", None),
        P("exp"),
        P(),
        P("exp", None),
        P("exp", None),
        P(None, None, "blk"),
        P("blk", None),
        P(("blk", "exp"), None, None),
        P(("blk", "exp"), None, None),
    )
    return jax.shard_map(
        per_device,
        mesh=mesh,
        in_specs=placed,
        out_specs=(P("exp", "blk"), P("exp", "blk", None, None)),
        check_vma=False,
    )
```

time: 529 us -> 212 us (0.40)
  waiting for transfers between devices: 300 us -> 0 us
  Pallas kernels: 0 us -> 138 us
  blocking collectives: 121 us -> 14.8 us
  matrix products: 35.3 us -> 20.4 us
  between operations: 15.1 us -> 1.83 us
  local copies, waits for them, and re-layouts: 33.3 us -> 24.8 us
  other arithmetic: 18.3 us -> 12.1 us
  starting transfers between devices: 5.7 us -> 0 us
    all_gather x5 -> x0, waiting for transfers between devices: 152 us -> none  [the longest x1 48.5 us: per_device(): shard_pages = lax.all_gather(pool_out, 'blk', axis=0, tiled=True)]
    pallas_call x0 -> x8, Pallas kernels: none -> 138 us  [the longest x4 44.6 us: gather_blk(): pl.pallas_call(functools.partial(gather_kernel, n), out_shape=jax.ShapeDt...]
    all_to_all x1 -> x0, blocking collectives: 121 us -> none  [per_device(): lax.all_to_all(outgoing, 'exp', split_axis=0, concat_axis=0, tiled=True)]
    all_to_all x1 -> x0, waiting for transfers between devices: 108 us -> none  [per_device(): lax.all_to_all(result.reshape(received.shape), 'exp', split_axis=0, conca...]
    reduce_scatter x1 -> x0, waiting for transfers between devices: 39.4 us -> none  [per_device(): lax.psum_scatter(layer_term, 'blk', scatter_dimension=1, tiled=True)]
    dot_general x11 -> x6, matrix products: 35.3 us -> 20.4 us  [columns_dot(): lax.dot_general(weight, inputs, (((0,), (0,)), ((), ())), preferred_eleme...]
    all_gather x0 -> x1, blocking collectives: none -> 14.8 us  [per_device(): all_shares = lax.all_gather(shares, 'exp', axis=1, tiled=True)]
    reduce_sum x6 -> x4, other arithmetic: 9.74 us -> 2.28 us  [the longest x2 1.51 us: normalize(): jnp.mean(values * values, axis=0, keepdims=True) + norm_eps]
  transfers between devices with their start and end apart: 7 -> 0, of which waited for: 7 -> 0; matrix products, arithmetic and copies ran while one was open for 3% -> 0% of each run, Pallas kernels for 0% -> 0%
where the time goes in v1:
time: 212 us
  Pallas kernels  138 us (65%)
  local copies, waits for them, and re-layouts  24.8 us (12%)
  matrix products  20.4 us (10%)
  blocking collectives  14.8 us (7%)
  other arithmetic  12.1 us (6%)
    pallas_call x4, Pallas kernels, gather_blk(): pl.pallas_call(functools.partial(gather_kernel, n), out_shape=jax.ShapeDt...  44.6 us
    pallas_call x1, Pallas kernels, gather_all(): pl.pallas_call(functools.partial(gather_all_kernel, n, g), out_shape=jax....  35.7 us
    pallas_call x1, Pallas kernels, reduce_all(): pl.pallas_call(functools.partial(reduce_all_kernel, n, g), out_shape=jax....  35.5 us
    dot_general x6, matrix products, columns_dot(): lax.dot_general(weight, inputs, (((0,), (0,)), ((), ())), preferred_eleme...  20.4 us
    all_gather x1, blocking collectives, per_device(): all_shares = lax.all_gather(shares, 'exp', axis=1, tiled=True)  14.8 us
    unnamed x30, local copies, waits for them, and re-layouts  12.9 us
    pallas_call x1, Pallas kernels, reduce_blk(): pl.pallas_call(functools.partial(reduce_kernel, n), out_shape=jax.ShapeDt...  12.5 us
    pallas_call x1, Pallas kernels, attend_local(): pl.pallas_call(attend_kernel, grid=(KV_HEADS,), out_shape=(jax.ShapeDtype...  9.71 us

profile of v1, /device:TPU:0, one launch (start us, length us, event | category | flops | bytes accessed | tf_op | source)
XLA Modules:
  0.0 211.9 jit_solution(1071625982192276210)
XLA Ops:
  3.5 14.8 %all_gather.3 = f32[8,1024]{1,0:T(8,128)S(1)} all-gather(f32[8,256]{1,0:T(8,128)S(1)} %select_reduce_fusion), channel_id=1, replica_groups=mesh['blk'=8,'exp'=4] {'exp'}, dimensions={1}, use_global_device_ids=true | all-gather | bytes 40960 | tf_op jit(solution)/shard_map/all_gather | solution.py:421
  18.8 0.9 copy-done.4
  19.7 11.3 %gather_blk1.1 = bf16[2560,256]{1,0:T(8,128)(2,1)S(1)} custom-call(bf16[320,256]{1,0:T(8,128)(2,1)S(1)} %bitcast.80), custom_call_target="tpu_custom_call" | custom-call | tf_op jit(solution)/shard_map/gather_blk1/pallas_call | solution.py:87
  32.3 15.1 %gather_blk2.1 = bf16[3584,256]{1,0:T(8,128)(2,1)S(1)} custom-call(bf16[448,256]{1,0:T(8,128)(2,1)S(1)} %fusion.29.x_ref), custom_call_target="tpu_custom_call" | custom-call | tf_op jit(solution)/shard_map/gather_blk2/pallas_call | solution.py:87
  50.4 2.8 %gather_fusion = bf16[512,1024]{1,0:T(8,128)(2,1)} fusion(bf16[256,1024]{1,0:T(8,128)(2,1)S(1)} %copy.25, s32[1024]{0:T(1024)S(1)} %pad_clamp_fusion), kind=kCustom, calls=%fused_computation | custom fusion | bytes 2099200 | tf_op jit(solution)/shard_map/gather | solution.py:451
  53.2 2.8 %broadcast_select_fusion = bf16[1,4,128,1024]{3,2,1,0:T(8,128)(2,1)} fusion(bf16[1,4,128,1024]{3,2,1,0:T(8,128)(2,1)} %bitcast.83, bf16[1,4,128,1024]{3,2,1,0:T(8,128)(2,1)} %param.18, pred[4,128]{1,0:T(4,128)(4,1)S(1)} %compare_and_fusion), kind=kLoop, calls=%fused_computation.38 | loop fusion | flops 524288 | bytes 3146240 | tf_op jit(solution)/shard_map/jit(_where)/select_n | solution.py:452
  56.3 9.7 %attend_local.1 = (f32[20,128,256]{2,1,0:T(8,128)S(1)}, f32[4,5,256]{2,1,0:T(8,128)S(1)}, f32[4,5,256]{2,1,0:T(8,128)S(1)}) custom-call(bf16[20,128,256]{2,1,0:T(8,128)(2,1)S(1)} %fusion.14.q_ref, bf16[512,1024]{1,0:T(8,128)(2,1)S(1)} %bitcast_select_fusion.k_ref.v_ref, bf16[512,1024]{1,0:T(8,128)(2,1)S(1)} %bitcast_select_fusion.k_ref.v_ref, ...), custom_call_target="tpu_custom_call" | custom-call | tf_op jit(solution)/shard_map/attend_local/pallas_call | solution.py:345
  66.1 1.5 copy-done.3
  67.6 6.4 %gather_blk3.1 = f32[320,256]{1,0:T(8,128)S(1)} custom-call(f32[40,256]{1,0:T(8,128)S(1)} %pad_maximum_fusion.1.x_ref), custom_call_target="tpu_custom_call" | custom-call | tf_op jit(solution)/shard_map/gather_blk3/pallas_call | solution.py:87
  74.2 2.2 %multiply_convert_fusion = bf16[20,128,256]{2,1,0:T(8,128)(2,1)S(1)} fusion(f32[20,128,256]{2,1,0:T(8,128)} %copy-done.3, f32[20,256]{1,0:T(8,128)S(1)} %exponential_divide_fusion), kind=kLoop, calls=%fused_computation.16 | loop fusion | flops 1310720 | bytes 3952640 | tf_op jit(solution)/shard_map/convert_element_type | solution.py:465
  76.4 12.5 %reduce_blk.1.x_ref = bf16[320,256]{1,0:T(8,128)(2,1)S(1)} custom-call(bf16[2560,256]{1,0:T(8,128)(2,1)S(1)} %bitcast.79), custom_call_target="tpu_custom_call" | custom-call | tf_op jit(solution)/shard_map/reduce_blk/pallas_call | solution.py:139
  88.9 11.7 %gather_blk5.1 = bf16[2560,256]{1,0:T(8,128)(2,1)S(1)} custom-call(bf16[320,256]{1,0:T(8,128)(2,1)S(1)} %reduce_blk.1.x_ref), custom_call_target="tpu_custom_call" | custom-call | tf_op jit(solution)/shard_map/gather_blk5/pallas_call | solution.py:87
  101.2 1.5 copy-done.8
  103.4 35.7 %gather_all.1 = bf16[2560,1024]{1,0:T(8,128)(2,1)S(1)} custom-call(bf16[320,256]{1,0:T(8,128)(2,1)S(1)} %fusion.28.x_ref), custom_call_target="tpu_custom_call" | custom-call | tf_op jit(solution)/shard_map/gather_all/pallas_call | solution.py:219
  139.2 1.1 fusion
  140.3 1.2 fusion.2
  141.6 1.2 fusion.21
  143.7 6.3 %fusion.10 = f32[768,1024]{0,1:T(8,128)} fusion(bf16[2560,1024]{1,0:T(8,128)(2,1)S(1)} %fusion.2, bf16[1,2560,768]{2,1,0:T(8,128)(2,1)S(1)} %copy-done.11), kind=kOutput, calls=%fused_computation.18 | convolution fusion | flops 4026531840 | bytes 12320768 | tf_op jit(solution)/shard_map/dot_general | solution.py:390
  150.0 2.4 %convolution_bitcast_fusion = f32[2560,256]{0,1:T(8,128)} fusion(bf16[384,2560]{1,0:T(8,128)(2,1)S(1)} %copy-done.9, f32[768,256]{0,1:T(8,128)S(1)} %fusion.21), kind=kOutput, calls=%fused_computation.8 | convolution fusion | flops 503906304 | bytes 5373952 | tf_op jit(solution)/shard_map/dot_general | solution.py:390
  152.3 3.2 %copy.29 = f32[2560,256]{1,0:T(8,128)} copy(f32[2560,256]{0,1:T(8,128)} %convolution_bitcast_fusion) | data formatting | bytes 5242880 | tf_op jit(solution)/shard_map/dot_general | solution.py:390
  155.6 4.5 %broadcast_in_dim.91 = f32[2560,4,256]{2,1,0:T(4,128)S(1)} broadcast(f32[2560,256]{1,0:T(8,128)} %copy.29), dimensions={0,2} | broadcast | bytes 13107200 | tf_op jit(solution)/shard_map/jit(_where)/broadcast_in_dim | solution.py:481
  160.1 6.6 %copy.33 = f32[320,8,4,256]{3,1,2,0:T(8,128)} copy(f32[320,8,4,256]{3,2,1,0:T(4,128)S(1)} %bitcast.81) | data formatting | bytes 20971520
  166.7 9.0 %fusion.3.x_ref = bf16[2560,1024]{1,0:T(8,128)(2,1)S(1)} fusion(f32[2560,1024]{1,0:T(8,128)} %bitcast.82, f32[1024]{0:T(1024)S(1)} %bitcast.91, pred[1024]{0:T(1024)(128)(4,1)S(1)} %broadcast_in_dim.89, bf16[1,384,2560]{2,1,0:T(8,128)(2,1)} %param.27, f32[768,1024]{0,1:T(8,128)} %fusion.10), kind=kOutput, calls=%fused_computation.7 | convolution fusion | flops 2026110976 | bytes 20845568 | tf_op jit(solution)/shard_map/dot_general | solution.py:390
  175.7 35.5 %reduce_all.1 = f32[320,256]{1,0:T(8,128)S(1)} custom-call(bf16[2560,1024]{1,0:T(8,128)(2,1)S(1)} %fusion.3.x_ref), custom_call_target="tpu_custom_call" | custom-call | tf_op jit(solution)/shard_map/reduce_all/pallas_call | solution.py:311
  (66 shorter events, 10.0 us)
Async XLA Ops:
  0.6 30.8 %copy-start = (bf16[2560,448]{0,1:T(8,128)(2,1)S(1)}, bf16[2560,448]{0,1:T(8,128)(2,1)}, u32[]{:S(2)}) copy-start(bf16[2560,448]{0,1:T(8,128)(2,1)} %param.16) | copy-start | bytes 6881284
  0.6 30.8 %copy-start.13 = (f32[2560]{0:T(1024)S(1)}, f32[2560]{0:T(1024)}, u32[]{:S(2)}) copy-start(f32[2560]{0:T(1024)} %param.15) | copy-start | bytes 30724
  18.8 0.9 copy-start.4
  47.4 1.3 copy-start.2
  49.2 1.0 slice-start
  53.2 2.8 %copy-start.6 = (bf16[512,1024]{1,0:T(8,128)(2,1)S(1)}, bf16[512,1024]{1,0:T(8,128)(2,1)}, u32[]{:S(2)}) copy-start(bf16[512,1024]{1,0:T(8,128)(2,1)} %gather_fusion) | copy-start | bytes 3145732
  53.2 2.8 %copy-start.7 = (bf16[1,4,128,1024]{3,2,1,0:T(8,128)(2,1)S(1)}, bf16[1,4,128,1024]{3,2,1,0:T(8,128)(2,1)}, u32[]{:S(2)}) copy-start(bf16[1,4,128,1024]{3,2,1,0:T(8,128)(2,1)} %param.18) | copy-start | bytes 3145732
  66.1 1.5 copy-start.3
  74.2 26.5 %copy-start.5 = (bf16[256,320]{0,1:T(8,128)(2,1)S(1)}, bf16[256,320]{0,1:T(8,128)(2,1)}, u32[]{:S(2)}) copy-start(bf16[256,320]{0,1:T(8,128)(2,1)} %param.14) | copy-start | bytes 491524
  74.2 26.5 %copy-start.12 = (bf16[2560,320]{0,1:T(8,128)(2,1)S(1)}, bf16[2560,320]{0,1:T(8,128)(2,1)}, u32[]{:S(2)}) copy-start(bf16[2560,320]{0,1:T(8,128)(2,1)} %param.17) | copy-start | bytes 4915204
  100.6 2.1 copy-start.8
  139.2 1.2 copy-start.10
  141.6 2.1 copy-start.11
  143.7 6.3 %copy-start.9 = (bf16[384,2560]{1,0:T(8,128)(2,1)S(1)}, bf16[384,2560]{1,0:T(8,128)(2,1)}, u32[]{:S(2)}) copy-start(bf16[384,2560]{1,0:T(8,128)(2,1)} %param.25) | copy-start | bytes 5898244
  166.7 45.3 %copy-start.1 = (bf16[2560,448]{0,1:T(8,128)(2,1)S(1)}, bf16[2560,448]{0,1:T(8,128)(2,1)}, u32[]{:S(2)}) copy-start(bf16[2560,448]{0,1:T(8,128)(2,1)} %param.16) | copy-start | bytes 6881284

commit v2 on v1

--- a/solution.py
+++ b/solution.py
@@ -149,120 +149,134 @@
     )(x)
 
 
-def gather_all_kernel(n, g, x_ref, o_ref, local_sem, zsend, zrecv, bsend, brecv, psend, precv):
+def experts_kernel(
+    n, g, eps, x_ref, gain_ref, share_ref, gu_hbm, down_hbm, sgu_hbm, sdown_hbm, o_ref,
+    full, part, shares, gu_raw, down_raw, sgu_raw, sdown_raw, gu, down, sgu, sdown,
+    normed, hid, act, sact, r1, s, r2, t, r3,
+    local_sem, wsem, zsend, zrecv, hsend, hrecv, bsend, brecv, psend, precv,
+    send1, recv1, send2, recv2, send3, recv3,
+):
     half = n // 2
     me, partner, peer = place(half)
     z = lax.axis_index("exp")
     rows, cols = x_ref.shape
+    width, ff = n * rows, act.shape[0]
 
     def zpeer(k):
         return (z + k + g) % g
 
-    def block(b, w):
-        return o_ref.at[
-            pl.ds(pl.multiple_of(b * rows, 16), rows), pl.ds(pl.multiple_of(w * cols, 128), cols)
-        ]
-
+    def span(w):
+        return pl.ds(pl.multiple_of(w * cols, 128), cols)
+
+    def at(b, w):
+        return pl.ds(pl.multiple_of(b * rows, 16), rows), span(w)
+
+    loads = [
+        pltpu.make_async_copy(src, dst, wsem.at[i])
+        for i, (src, dst) in enumerate(
+            [(gu_hbm, gu_raw), (down_hbm, down_raw), (sgu_hbm, sgu_raw), (sdown_hbm, sdown_raw)]
+        )
+    ]
+    for load in loads:
+        load.start()
     greet(
         [{"exp": zpeer(k)} for k in range(1, g)]
         + [{"blk": peer(k)} for k in range(1, half)]
         + [{"blk": partner}]
     )
     along = [
-        remote(x_ref, block(me, z), zsend.at[k], zrecv.at[k], exp=zpeer(k)) for k in range(1, g)
+        remote(x_ref, full.at[at(me, z)], zsend.at[k], zrecv.at[k], exp=zpeer(k))
+        for k in range(1, g)
     ]
-    for copy in along:
-        copy.start()
-    own = pltpu.make_async_copy(x_ref, block(me, z), local_sem)
-    own.start()
-    outs, passed = {}, []
+    told = [
+        remote(share_ref, shares.at[:, span(z)], hsend.at[k], hrecv.at[k], exp=zpeer(k))
+        for k in range(1, g)
+    ]
+    own = pltpu.make_async_copy(x_ref, full.at[at(me, z)], local_sem.at[0])
+    own_share = pltpu.make_async_copy(share_ref, shares.at[:, span(z)], local_sem.at[1])
+    outs, passed, first, second, third = {}, {}, {}, {}, {}
+    order = list(range(1, half)) + [0]
 
     def spread(kz):
         w = zpeer(-kz)
-        src = x_ref if kz == 0 else block(me, w)
+        if kz:
+            along[kz - 1].wait_recv()
+        src = x_ref if kz == 0 else full.at[at(me, w)]
         for k in range(1, half):
-            outs[kz, k] = remote(src, block(me, w), bsend.at[kz, k], brecv.at[kz, k], blk=peer(k))
+            outs[kz, k] = remote(
+                src, full.at[at(me, w)], bsend.at[kz, k], brecv.at[kz, k], blk=peer(k)
+            )
             outs[kz, k].start()
-        copy = remote(src, block(me, w), psend.at[kz, 0], precv.at[kz, 0], blk=partner)
-        copy.start()
-        passed.append(copy)
+        passed[kz, 0] = remote(
+            src, full.at[at(me, w)], psend.at[kz, 0], precv.at[kz, 0], blk=partner
+        )
+        passed[kz, 0].start()
 
     def relay(kz):
         w = zpeer(-kz)
         for k in range(1, half):
             outs[kz, k].wait_recv()
-            here = block(peer(-k), w)
-            copy = remote(here, here, psend.at[kz, k], precv.at[kz, k], blk=partner)
-            copy.start()
-            passed.append(copy)
-
-    spread(0)
-    for kz in range(1, g):
-        along[kz - 1].wait_recv()
-        spread(kz)
-        relay(kz - 1)
-    relay(g - 1)
-    for copy in along + list(outs.values()):
-        copy.wait_send()
-    for copy in passed:
-        copy.wait()
-    own.wait()
-
-
-def gather_all(x, collective_id):
-    n, g = lax.axis_size("blk"), lax.axis_size("exp")
-    half = n // 2
-    if n * g > 32:
-        along = lax.all_gather(x, "exp", axis=1, tiled=True)
-        return lax.all_gather(along, "blk", axis=0, tiled=True)
-    dma = pltpu.SemaphoreType.DMA
-    return pl.pallas_call(
-        functools.partial(gather_all_kernel, n, g),
-        out_shape=jax.ShapeDtypeStruct((n * x.shape[0], g * x.shape[1]), x.dtype),
-        in_specs=[pl.BlockSpec(memory_space=VM)],
-        out_specs=pl.BlockSpec(memory_space=VM),
-        scratch_shapes=[dma] + [dma((g,))] * 2 + [dma((g, half))] * 4,
-        compiler_params=pltpu.CompilerParams(
-            collective_id=collective_id, has_side_effects=True, vmem_limit_bytes=40 << 20
-        ),
-        name="gather_all",
-    )(x)
-
-
-def reduce_all_kernel(
-    n, g, x_ref, o_ref, r1, s, r2, t, r3, send1, recv1, send2, recv2, send3, recv3
-):
-    half = n // 2
-    me, partner, peer = place(half)
-    z = lax.axis_index("exp")
-    rows, cols = o_ref.shape
-
-    def zpeer(k):
-        return (z + k + g) % g
-
-    def at(b, w):
-        return (
-            pl.ds(pl.multiple_of(b * rows, 16), rows),
-            pl.ds(pl.multiple_of(w * cols, 128), cols),
-        )
-
-    greet(
-        [{"exp": zpeer(k)} for k in range(1, g)]
-        + [{"blk": peer(k)} for k in range(1, half)]
-        + [{"blk": partner}]
-    )
-    chunks = list(range(1, g)) + [0]
-    order = list(range(1, half)) + [0]
-    first, second, third = {}, {}, {}
-    for kz in chunks:
+            here = full.at[at(peer(-k), w)]
+            passed[kz, k] = remote(here, here, psend.at[kz, k], precv.at[kz, k], blk=partner)
+            passed[kz, k].start()
+
+    def turn(i, src, dst, step):
+        loads[i].wait()
+
+        @pl.loop(0, src.shape[1] // step)
+        def _(j):
+            c = pl.ds(pl.multiple_of(j * step, 128), step)
+            dst[c, :] = src[:, c].T
+
+    def arrive(kz):
+        for k in range(half):
+            passed[kz, k].wait_recv()
+
+    def norm(kz):
+        w = zpeer(-kz)
+        tile = 256
+
+        def add(j, total):
+            v = full[pl.ds(pl.multiple_of(j * tile, 16), tile), span(w)].astype(F32)
+            return total + jnp.sum(v * v, axis=0, keepdims=True)
+
+        total = lax.fori_loop(0, width // tile, add, jnp.zeros((1, cols), F32))
+        inv = lax.rsqrt(total * (1.0 / width) + eps)
+
+        @pl.loop(0, width // tile)
+        def _(j):
+            r = pl.ds(pl.multiple_of(j * tile, 16), tile)
+            normed[r, :] = (full[r, span(w)].astype(F32) * inv * gain_ref[r, :]).astype(BF16)
+
+    def hidden_units(weight, out, factor):
+        tile = 256
+
+        @pl.loop(0, 2 * ff // tile)
+        def _(j):
+            r = pl.ds(pl.multiple_of(j * tile, 16), tile)
+            hid[r, :] = jnp.dot(weight[r, :], normed[...], preferred_element_type=F32)
+
+        gate = hid[pl.ds(0, ff), :]
+        out[...] = (gate / (1.0 + jnp.exp(-gate)) * hid[pl.ds(ff, ff), :] * factor).astype(BF16)
+
+    def expert(kz):
+        w = zpeer(-kz)
+        row = (me * g + z) // SPLIT
+        hidden_units(gu, act, shares[pl.ds(row, 1), span(w)])
+        tile = 256
+
+        @pl.loop(0, width // tile)
+        def _(j):
+            r = pl.ds(pl.multiple_of(j * tile, 16), tile)
+            y = jnp.dot(down[r, :], act[...], preferred_element_type=F32)
+            if kz == 0:
+                y += jnp.dot(sdown[r, :], sact[...], preferred_element_type=F32)
+            part[r, span(w)] = y.astype(BF16)
+
         for k in order:
             other = peer(k) + partner - me
             first[kz, k] = remote(
-                x_ref.at[at(other, zpeer(kz))],
-                r1.at[kz, k],
-                send1.at[kz, k],
-                recv1.at[kz, k],
-                blk=partner,
+                part.at[at(other, w)], r1.at[kz, k], send1.at[kz, k], recv1.at[kz, k], blk=partner
             )
             first[kz, k].start()
 
@@ -270,7 +284,7 @@
         for k in order:
             first[kz, k].wait_recv()
             if k:
-                mine = x_ref[at(peer(k), zpeer(kz))].astype(F32)
+                mine = part[at(peer(k), zpeer(-kz))].astype(F32)
                 s[kz, k] = (mine + r1[kz, k].astype(F32)).astype(BF16)
                 second[kz, k] = remote(
                     s.at[kz, k], r2.at[kz, k], send2.at[kz, k], recv2.at[kz, k], blk=peer(k)
@@ -278,50 +292,114 @@
                 second[kz, k].start()
 
     def finish(kz):
-        total = x_ref[at(me, zpeer(kz))].astype(F32) + r1[kz, 0].astype(F32)
+        total = part[at(me, zpeer(-kz))].astype(F32) + r1[kz, 0].astype(F32)
         for k in range(1, half):
             second[kz, k].wait_recv()
             total += r2[kz, k].astype(F32)
         if kz:
             t[kz] = total.astype(BF16)
-            third[kz] = remote(t.at[kz], r3.at[kz], send3.at[kz], recv3.at[kz], exp=zpeer(kz))
+            third[kz] = remote(t.at[kz], r3.at[kz], send3.at[kz], recv3.at[kz], exp=zpeer(-kz))
             third[kz].start()
         return total
 
-    for kz in chunks:
-        pair(kz)
-    for kz in chunks:
-        total = finish(kz)
+    spread(0)
+    for copy in along + told:
+        copy.start()
+    own.start()
+    own_share.start()
+    turn(0, gu_raw, gu, 256)
+    spread(1)
+    relay(0)
+    turn(1, down_raw, down, 512)
+    spread(2)
+    relay(1)
+    own.wait()
+    own_share.wait()
+    turn(2, sgu_raw, sgu, 256)
+    arrive(0)
+    spread(3)
+    relay(2)
+    norm(0)
+    hidden_units(sgu, sact, 1.0)
+    for copy in told:
+        copy.wait()
+    arrive(1)
+    norm(1)
+    expert(1)
+    relay(3)
+    turn(3, sdown_raw, sdown, 512)
+    pair(1)
+    arrive(2)
+    norm(2)
+    expert(2)
+    pair(2)
+    arrive(3)
+    norm(3)
+    expert(3)
+    pair(3)
+    norm(0)
+    expert(0)
+    pair(0)
+    for kz in range(1, g):
+        finish(kz)
+    total = finish(0)
     for kz in range(1, g):
         third[kz].wait_recv()
         total += r3[kz].astype(F32)
     o_ref[...] = total
-    for copy in list(first.values()) + list(second.values()) + list(third.values()):
+    for copy in along + [c for d in (outs, passed, first, second, third) for c in d.values()]:
         copy.wait_send()
 
 
-def reduce_all(x, collective_id):
+def experts_fused(x, gain, share, gate_up, down, shared_gate_up, shared_down, collective_id):
     n, g = lax.axis_size("blk"), lax.axis_size("exp")
     half = n // 2
-    if n * g > 32:
-        part = lax.psum_scatter(x, "blk", scatter_dimension=0, tiled=True)
-        return lax.psum_scatter(part, "exp", scatter_dimension=1, tiled=True).astype(F32)
     dma = pltpu.SemaphoreType.DMA
-    rows, cols = x.shape[0] // n, x.shape[1] // g
+    rows, cols = x.shape
+    width, ff = n * rows, down.shape[0]
+    weights = [gate_up, down, shared_gate_up, shared_down]
     return pl.pallas_call(
-        functools.partial(reduce_all_kernel, n, g),
+        functools.partial(experts_kernel, n, g, norm_eps),
         out_shape=jax.ShapeDtypeStruct((rows, cols), F32),
-        in_specs=[pl.BlockSpec(memory_space=VM)],
+        in_specs=[pl.BlockSpec(memory_space=VM)] * 3 + [pl.BlockSpec(memory_space=pl.ANY)] * 4,
         out_specs=pl.BlockSpec(memory_space=VM),
-        scratch_shapes=[VM((g, half, rows, cols), BF16)] * 3
+        scratch_shapes=[VM((width, g * cols), BF16)] * 2
+        + [VM((share.shape[0], g * cols), F32)]
+        + [VM(w.shape, BF16) for w in weights]
+        + [VM(w.shape[::-1], BF16) for w in weights]
+        + [VM((width, cols), BF16), VM((2 * ff, cols), F32)]
+        + [VM((ff, cols), BF16)] * 2
+        + [VM((g, half, rows, cols), BF16)] * 3
         + [VM((g, rows, cols), BF16)] * 2
-        + [dma((g, half))] * 4
+        + [dma((2,)), dma((4,))]
+        + [dma((g,))] * 4
+        + [dma((g, half))] * 8
         + [dma((g,))] * 2,
         compiler_params=pltpu.CompilerParams(
-            collective_id=collective_id, has_side_effects=True, vmem_limit_bytes=40 << 20
+            collective_id=collective_id, has_side_effects=True, vmem_limit_bytes=58 << 20
         ),
-        name="reduce_all",
-    )(x)
+        name="experts_fused",
+    )(x, gain[:, None], share, *weights)
+
+
+def experts_wide(x, gain, share, gate_up, down, shared_gate_up, shared_down):
+    g, z, cols = lax.axis_size("exp"), lax.axis_index("exp"), x.shape[1]
+    ff = down.shape[0]
+    row = (lax.axis_index("blk") * g + z) // SPLIT
+    factor = lax.dynamic_slice_in_dim(lax.all_gather(share, "exp", axis=1, tiled=True), row, 1, 0)
+    along = lax.all_gather(x, "exp", axis=1, tiled=True)
+    ffn_in = normalize(lax.all_gather(along, "blk", axis=0, tiled=True), gain)
+    own_in = lax.dynamic_slice_in_dim(ffn_in, z * cols, cols, 1)
+    shared_ff = shared_down.shape[0]
+    both = columns_dot(shared_gate_up, own_in)
+    shared_act = (jax.nn.silu(both[:shared_ff]) * both[shared_ff:]).astype(BF16)
+    gu = columns_dot(gate_up, ffn_in)
+    act = (jax.nn.silu(gu[:ff]) * gu[ff:] * factor).astype(BF16)
+    layer = columns_dot(down, act)
+    own = lax.dynamic_slice_in_dim(layer, z * cols, cols, 1) + columns_dot(shared_down, shared_act)
+    layer = lax.dynamic_update_slice_in_dim(layer, own, z * cols, 1).astype(BF16)
+    part = lax.psum_scatter(layer, "blk", scatter_dimension=0, tiled=True)
+    return lax.psum_scatter(part, "exp", scatter_dimension=1, tiled=True).astype(F32)
 
 
 def attend_kernel(q_ref, k_ref, v_ref, kpos_ref, qpos_ref, acc_ref, max_ref, sum_ref):
@@ -409,7 +487,6 @@
     blocks = lax.axis_size("blk")
     groups = lax.axis_size("exp")
     block_index = lax.axis_index("blk")
-    group_index = lax.axis_index("exp")
     model_width = hidden.shape[1] * blocks
     query_width = HEADS * HEAD_DIM
     key_width = KV_HEADS * HEAD_DIM
@@ -418,9 +495,6 @@
     experts = jnp.arange(expert_count, dtype=jnp.int32)
     hits = route_ids.T[None] == experts[:, None, None]
     shares = jnp.sum(jnp.where(hits, route_weights.T[None], 0.0), axis=1)
-    all_shares = lax.all_gather(shares, "exp", axis=1, tiled=True)
-    own_expert = (block_index * groups + group_index) // SPLIT
-    share = lax.dynamic_slice_in_dim(all_shares, own_expert, 1, 0)
 
     hidden_t = hidden.T
     attn_in = normalize(gather_blk(hidden_t, 1), attn_gain)
@@ -467,19 +541,20 @@
     attended = columns_dot(out_weight, attention)
     mixed = (hidden_t.astype(F32) + attended).astype(BF16)
 
-    ffn_in = normalize(gather_all(mixed, 6), ffn_gain)
-    own_in = lax.dynamic_slice_in_dim(ffn_in, group_index * NEW, NEW, 1)
     shared_cols = shared_gate_up.shape[2]
-    gate_up = columns_dot(shared_gate_up.reshape(model_width, 2 * shared_cols), own_in)
-    shared_act = (jax.nn.silu(gate_up[:shared_cols]) * gate_up[shared_cols:]).astype(BF16)
-    shared_term = columns_dot(shared_down, shared_act)
-
-    expert_gu = columns_dot(expert_gate_up[0], ffn_in)
-    activated = (jax.nn.silu(expert_gu[:FF_PART]) * expert_gu[FF_PART:]).astype(BF16)
-    result = columns_dot(expert_down[0], activated) * share
-    mine = (jnp.arange(groups, dtype=jnp.int32) == group_index)[None, :, None]
-    layer = result.reshape(model_width, groups, NEW) + jnp.where(mine, shared_term[:, None, :], 0.0)
-    summed = reduce_all(layer.astype(BF16).reshape(model_width, groups * NEW), 7)
+    operands = (
+        mixed,
+        ffn_gain,
+        shares,
+        expert_gate_up[0],
+        expert_down[0],
+        shared_gate_up.reshape(model_width, 2 * shared_cols),
+        shared_down,
+    )
+    if blocks * groups > 32:
+        summed = experts_wide(*operands)
+    else:
+        summed = experts_fused(*operands, 6)
     hidden_out = (mixed.astype(F32) + summed).astype(BF16)
     return (hidden_out.T, pool_out[None])
 

time: 212 us -> 178 us (0.84)
  matrix products: 20.4 us -> 2.13 us
  blocking collectives: 14.8 us -> 0 us
  Pallas kernels: 138 us -> 148 us
  local copies, waits for them, and re-layouts: 24.8 us -> 14.8 us
    dot_general x6 -> x2, matrix products: 20.4 us -> 2.13 us  [columns_dot(): lax.dot_general(weight, inputs, (((0,), (0,)), ((), ())), preferred_eleme...]
    all_gather x1 -> x0, blocking collectives: 14.8 us -> none  [per_device(): all_shares = lax.all_gather(shares, 'exp', axis=1, tiled=True)]
    pallas_call x2 -> x1, Pallas kernels: 71.2 us -> 79.5 us  [experts_fused(): pl.pallas_call(functools.partial(experts_kernel, n, g, norm_eps), out_sha...]
    unnamed x30 -> x41, local copies, waits for them, and re-layouts: 12.9 us -> 9.33 us
    dot_general x1 -> x0, local copies, waits for them, and re-layouts: 3.24 us -> none  [columns_dot(): lax.dot_general(weight, inputs, (((0,), (0,)), ((), ())), preferred_eleme...]
    broadcast_in_dim x3 -> x1, local copies, waits for them, and re-layouts: 4.56 us -> 1.45 us  [experts_fused(): gain[:, None]]
    pallas_call x4, Pallas kernels: 44.6 us -> 46.8 us  [gather_blk(): pl.pallas_call(functools.partial(gather_kernel, n), out_shape=jax.ShapeDt...]
where the time goes in v2:
time: 178 us
  Pallas kernels  148 us (83%)
  local copies, waits for them, and re-layouts  14.8 us (8%)
  other arithmetic  10.7 us (6%)
  matrix products  2.13 us (1%)
    pallas_call x1, Pallas kernels, experts_fused(): pl.pallas_call(functools.partial(experts_kernel, n, g, norm_eps), out_sha...  79.5 us
    pallas_call x4, Pallas kernels, gather_blk(): pl.pallas_call(functools.partial(gather_kernel, n), out_shape=jax.ShapeDt...  46.8 us
    pallas_call x1, Pallas kernels, reduce_blk(): pl.pallas_call(functools.partial(reduce_kernel, n), out_shape=jax.ShapeDt...  12.4 us
    pallas_call x1, Pallas kernels, attend_local(): pl.pallas_call(attend_kernel, grid=(KV_HEADS,), out_shape=(jax.ShapeDtype...  9.72 us
    unnamed x41, local copies, waits for them, and re-layouts  9.33 us

profile of v2, /device:TPU:0, one launch (start us, length us, event | category | flops | bytes accessed | tf_op | source)
XLA Modules:
  0.0 177.8 jit_solution(5908320615569488797)
XLA Ops:
  1.8 0.9 copy-done.4
  2.7 13.3 %gather_blk1.1 = bf16[2560,256]{1,0:T(8,128)(2,1)S(1)} custom-call(bf16[320,256]{1,0:T(8,128)(2,1)S(1)} %bitcast.58), custom_call_target="tpu_custom_call" | custom-call | tf_op jit(solution)/shard_map/gather_blk1/pallas_call | solution.py:87
  16.4 0.9 fusion.13.x_ref
  17.3 15.1 %gather_blk2.1 = bf16[3584,256]{1,0:T(8,128)(2,1)S(1)} custom-call(bf16[448,256]{1,0:T(8,128)(2,1)S(1)} %fusion.13.x_ref), custom_call_target="tpu_custom_call" | custom-call | tf_op jit(solution)/shard_map/gather_blk2/pallas_call | solution.py:87
  33.5 0.8 copy-done.7
  35.1 2.8 %gather_fusion = bf16[512,1024]{1,0:T(8,128)(2,1)} fusion(bf16[256,1024]{1,0:T(8,128)(2,1)S(1)} %copy.22, s32[1024]{0:T(1024)S(1)} %pad_clamp_fusion), kind=kCustom, calls=%fused_computation | custom fusion | bytes 2099200 | tf_op jit(solution)/shard_map/gather | solution.py:525
  38.0 1.8 %bitcast_select_fusion.k_ref.v_ref = bf16[512,1024]{1,0:T(8,128)(2,1)S(1)} fusion(bf16[512,1024]{1,0:T(8,128)(2,1)} %gather_fusion, bf16[1,4,128,1024]{3,2,1,0:T(8,128)(2,1)} %param.18, pred[512]{0:T(512)(128)(4,1)S(1)} %fusion.24), kind=kLoop, calls=%fused_computation.20 | loop fusion | flops 524288 | bytes 3146240 | tf_op jit(solution)/shard_map/jit(_where)/select_n | solution.py:526
  39.9 1.2 fusion.3.q_ref
  41.1 0.9 copy.23.kpos_ref
  42.0 1.3 copy-done.1
  43.3 0.9 copy-done.3
  44.3 9.7 %attend_local.1 = (f32[20,128,256]{2,1,0:T(8,128)S(1)}, f32[4,5,256]{2,1,0:T(8,128)S(1)}, f32[4,5,256]{2,1,0:T(8,128)S(1)}) custom-call(bf16[20,128,256]{2,1,0:T(8,128)(2,1)S(1)} %copy-done.1, bf16[512,1024]{1,0:T(8,128)(2,1)S(1)} %bitcast_select_fusion.k_ref.v_ref, bf16[512,1024]{1,0:T(8,128)(2,1)S(1)} %bitcast_select_fusion.k_ref.v_ref, ...), custom_call_target="tpu_custom_call" | custom-call | tf_op jit(solution)/shard_map/attend_local/pallas_call | solution.py:423
  54.0 1.5 copy-done.2
  55.6 6.7 %gather_blk3.1 = f32[320,256]{1,0:T(8,128)S(1)} custom-call(f32[40,256]{1,0:T(8,128)S(1)} %pad_maximum_fusion.1.x_ref), custom_call_target="tpu_custom_call" | custom-call | tf_op jit(solution)/shard_map/gather_blk3/pallas_call | solution.py:87
  62.4 2.0 %multiply_convert_fusion = bf16[20,128,256]{2,1,0:T(8,128)(2,1)S(1)} fusion(f32[20,128,256]{2,1,0:T(8,128)} %copy-done.2, f32[20,256]{1,0:T(8,128)S(1)} %exponential_divide_fusion), kind=kLoop, calls=%fused_computation.6 | loop fusion | flops 1310720 | bytes 3952640 | tf_op jit(solution)/shard_map/convert_element_type | solution.py:539
  64.5 12.4 %reduce_blk.1.x_ref = bf16[320,256]{1,0:T(8,128)(2,1)S(1)} custom-call(bf16[2560,256]{1,0:T(8,128)(2,1)S(1)} %bitcast.57), custom_call_target="tpu_custom_call" | custom-call | tf_op jit(solution)/shard_map/reduce_blk/pallas_call | solution.py:139
  76.9 11.7 %gather_blk5.1 = bf16[2560,256]{1,0:T(8,128)(2,1)S(1)} custom-call(bf16[320,256]{1,0:T(8,128)(2,1)S(1)} %reduce_blk.1.x_ref), custom_call_target="tpu_custom_call" | custom-call | tf_op jit(solution)/shard_map/gather_blk5/pallas_call | solution.py:87
  88.7 1.3 fusion.12.x_ref
  89.9 0.9 copy-done.12
  90.8 2.5 %copy.27 = bf16[320,8,2,384]{3,1,2,0:T(8,128)(2,1)} copy(bf16[320,8,2,384]{3,2,1,0:T(2,128)(2,1)S(1)} %bitcast.62) | data formatting | bytes 7864320
  93.4 1.5 broadcast_in_dim.63.gain_ref
  95.4 79.5 %experts_fused.1 = f32[320,256]{1,0:T(8,128)} custom-call(bf16[320,256]{1,0:T(8,128)(2,1)} %fusion.12.x_ref, f32[2560,1]{1,0:T(8,128)} %broadcast_in_dim.63.gain_ref, f32[8,256]{1,0:T(8,128)} %select_reduce_fusion.share_ref, bf16[2560,768]{1,0:T(8,128)(2,1)} %bitcast.63, bf16[384,2560]{1,0:T(8,128)(2,1)} %bitcast.64, bf16[2560,768]{1,0:T(8,128)(2,1)} %bitcast.59, ...), custom_call_target="tpu_custom_call" | custom-call | tf_op jit(solution)/shard_map/experts_fused/pallas_call | solution.py:361
  174.9 1.7 fusion.19
  176.7 1.1 broadcast_select_fusion
  (62 shorter events, 3.6 us)
Async XLA Ops:
  0.6 15.8 %copy-start = (bf16[2560,448]{0,1:T(8,128)(2,1)S(1)}, bf16[2560,448]{0,1:T(8,128)(2,1)}, u32[]{:S(2)}) copy-start(bf16[2560,448]{0,1:T(8,128)(2,1)} %param.16) | copy-start | bytes 6881284
  0.6 15.8 %copy-start.18 = (f32[2560]{0:T(1024)S(1)}, f32[2560]{0:T(1024)}, u32[]{:S(2)}) copy-start(f32[2560]{0:T(1024)} %param.15) | copy-start | bytes 30724
  1.8 0.9 copy-start.4
  33.5 0.9 copy-start.7
  33.5 1.1 copy-start.9
  33.5 1.4 copy-start.19
  37.9 1.9 %copy-start.8 = (bf16[24,64,256]{2,1,0:T(8,128)(2,1)S(1)}, bf16[24,64,256]{2,1,0:T(8,128)(2,1)}, u32[]{:S(2)}) copy-start(bf16[24,64,256]{2,1,0:T(8,128)(2,1)} %copy-done.7) | copy-start | bytes 2359300
  37.9 2.0 %copy-start.10 = (bf16[24,64,256]{2,1,0:T(8,128)(2,1)S(1)}, bf16[24,64,256]{2,1,0:T(8,128)(2,1)}, u32[]{:S(2)}) copy-start(bf16[24,64,256]{2,1,0:T(8,128)(2,1)} %copy-done.9) | copy-start | bytes 2359300
  42.0 1.3 copy-start.1
  43.3 0.9 copy-start.3
  54.0 1.5 copy-start.2
  64.5 24.2 %copy-start.5 = (bf16[256,320]{0,1:T(8,128)(2,1)S(1)}, bf16[256,320]{0,1:T(8,128)(2,1)}, u32[]{:S(2)}) copy-start(bf16[256,320]{0,1:T(8,128)(2,1)} %param.14) | copy-start | bytes 491524
  64.5 24.2 %copy-start.17 = (bf16[2560,320]{0,1:T(8,128)(2,1)S(1)}, bf16[2560,320]{0,1:T(8,128)(2,1)}, u32[]{:S(2)}) copy-start(bf16[2560,320]{0,1:T(8,128)(2,1)} %param.17) | copy-start | bytes 4915204
  88.6 2.2 %copy-start.12 = (bf16[2560,2,384]{2,1,0:T(2,128)(2,1)S(1)}, bf16[2560,2,384]{2,1,0:T(2,128)(2,1)}, u32[]{:S(2)}) copy-start(bf16[2560,2,384]{2,1,0:T(2,128)(2,1)} %param.24) | copy-start | bytes 11796484
  90.8 2.5 %copy-start.14 = (f32[2560]{0:T(1024)S(1)}, f32[2560]{0:T(1024)}, u32[]{:S(2)}) copy-start(f32[2560]{0:T(1024)} %param.21) | copy-start | bytes 30724
  90.8 4.0 %copy-start.15 = (f32[256,6]{0,1:T(8,128)S(1)}, f32[256,6]{0,1:T(8,128)}, u32[]{:S(2)}) copy-start(f32[256,6]{0,1:T(8,128)} %param.23) | copy-start | bytes 18436
  90.8 4.0 %copy-start.16 = (s32[256,6]{0,1:T(8,128)S(1)}, s32[256,6]{0,1:T(8,128)}, u32[]{:S(2)}) copy-start(s32[256,6]{0,1:T(8,128)} %param.22) | copy-start | bytes 18436
  95.4 79.5 %copy-start.13 = (bf16[320,256]{1,0:T(8,128)(2,1)S(1)}, bf16[320,256]{1,0:T(8,128)(2,1)}, u32[]{:S(2)}) copy-start(bf16[320,256]{1,0:T(8,128)(2,1)} %fusion.12.x_ref) | copy-start | bytes 491524
  95.4 81.3 %copy-start.6 = (bf16[512,1024]{1,0:T(8,128)(2,1)S(1)}, bf16[512,1024]{1,0:T(8,128)(2,1)}, u32[]{:S(2)}) copy-start(bf16[512,1024]{1,0:T(8,128)(2,1)} %gather_fusion) | copy-start | bytes 3145732
  95.4 81.3 %copy-start.11 = (bf16[1,4,128,1024]{3,2,1,0:T(8,128)(2,1)S(1)}, bf16[1,4,128,1024]{3,2,1,0:T(8,128)(2,1)}, u32[]{:S(2)}) copy-start(bf16[1,4,128,1024]{3,2,1,0:T(8,128)(2,1)} %param.18) | copy-start | bytes 3145732

commit v3 on v2

--- a/solution.py
+++ b/solution.py
@@ -51,7 +51,7 @@
     return me, partner, peer
 
 
-def gather_kernel(n, x_ref, o_ref, local_sem, send, recv, fsend, frecv):
+def gather_kernel(n, x_ref, o_ref, local_sem, send, recv, fsend, frecv, meet=True):
     half = n // 2
     me, partner, peer = place(half)
     rows = x_ref.shape[0]
@@ -59,7 +59,8 @@
     def block(b):
         return o_ref.at[pl.ds(pl.multiple_of(b * rows, 8), rows), :]
 
-    greet([{"blk": peer(k)} for k in range(1, half)] + [{"blk": partner}])
+    if meet:
+        greet([{"blk": peer(k)} for k in range(1, half)] + [{"blk": partner}])
     outs = [remote(x_ref, block(me), send.at[k], recv.at[k], blk=peer(k)) for k in range(1, half)]
     for copy in outs:
         copy.start()
@@ -97,7 +98,7 @@
     )(x)
 
 
-def reduce_kernel(n, x_ref, o_ref, r1, s, r2, send1, recv1, send2, recv2):
+def reduce_kernel(n, x_ref, o_ref, r1, s, r2, send1, recv1, send2, recv2, meet=True):
     half = n // 2
     me, partner, peer = place(half)
     rows = o_ref.shape[0]
@@ -105,7 +106,8 @@
     def block(b):
         return pl.ds(pl.multiple_of(b * rows, 16), rows)
 
-    greet([{"blk": peer(k)} for k in range(1, half)] + [{"blk": partner}])
+    if meet:
+        greet([{"blk": peer(k)} for k in range(1, half)] + [{"blk": partner}])
     order = list(range(1, half)) + [0]
     first = {}
     for k in order:
@@ -131,21 +133,30 @@
         copy.wait_send()
 
 
-def reduce_blk(x, collective_id):
+def sum_kernel(n, x_ref, o_ref, own, *scratch):
+    reduce_kernel(n, x_ref, own, *scratch[:7])
+    gather_kernel(n, own, o_ref, *scratch[7:], meet=False)
+
+
+def sum_blk(x, collective_id):
     n = lax.axis_size("blk")
     half = n // 2
     dma = pltpu.SemaphoreType.DMA
     rows, cols = x.shape[0] // n, x.shape[1]
     return pl.pallas_call(
-        functools.partial(reduce_kernel, n),
-        out_shape=jax.ShapeDtypeStruct((rows, cols), BF16),
+        functools.partial(sum_kernel, n),
+        out_shape=jax.ShapeDtypeStruct(x.shape, BF16),
         in_specs=[pl.BlockSpec(memory_space=VM)],
         out_specs=pl.BlockSpec(memory_space=VM),
-        scratch_shapes=[VM((half, rows, cols), BF16)] * 3 + [dma((half,))] * 4,
+        scratch_shapes=[VM((rows, cols), BF16)]
+        + [VM((half, rows, cols), BF16)] * 3
+        + [dma((half,))] * 4
+        + [dma]
+        + [dma((half,))] * 4,
         compiler_params=pltpu.CompilerParams(
             collective_id=collective_id, has_side_effects=True, vmem_limit_bytes=32 << 20
         ),
-        name="reduce_blk",
+        name="sum_blk",
     )(x)
 
 
@@ -405,12 +416,13 @@
 def attend_kernel(q_ref, k_ref, v_ref, kpos_ref, qpos_ref, acc_ref, max_ref, sum_ref):
     allowed = kpos_ref[...] <= qpos_ref[...]
     keys, vals = k_ref[...], v_ref[...]
+    scale = 1.0 / math.sqrt(HEAD_DIM)
     for h in range(GROUP):
-        scores = jnp.dot(keys, q_ref[h], preferred_element_type=F32) * (1.0 / math.sqrt(HEAD_DIM))
+        scores = jnp.dot(keys, q_ref[h], preferred_element_type=F32)
         scores = jnp.where(allowed, scores, -1e30)
         peak = jnp.max(scores, axis=0, keepdims=True)
-        weights = jnp.where(allowed, jnp.exp(scores - peak), 0.0)
-        max_ref[0, pl.ds(h, 1), :] = peak
+        weights = jnp.exp2((scores - peak) * (scale * math.log2(math.e)))
+        max_ref[0, pl.ds(h, 1), :] = peak * scale
         sum_ref[0, pl.ds(h, 1), :] = jnp.sum(weights, axis=0, keepdims=True)
         acc_ref[h] = lax.dot_general(
             vals, weights.astype(BF16), (((0,), (0,)), ((), ())), preferred_element_type=F32
@@ -537,7 +549,7 @@
     whole = jnp.sum(all_stats[:, 1] * jnp.exp(all_stats[:, 0] - top[None]), axis=0)
     factor = jnp.exp(stats[:HEADS] - top) / whole
     scaled = (acc * factor[:, None, :]).astype(BF16).reshape(query_width, NEW)
-    attention = gather_blk(reduce_blk(scaled, 4), 5)
+    attention = sum_blk(scaled, 4)
     attended = columns_dot(out_weight, attention)
     mixed = (hidden_t.astype(F32) + attended).astype(BF16)
 

time: 178 us -> 176 us (0.989)
  Pallas kernels: 148 us -> 146 us
    pallas_call x4 -> x3, Pallas kernels: 46.8 us -> 35.1 us  [gather_blk(): pl.pallas_call(functools.partial(gather_kernel, n), out_shape=jax.ShapeDt...]
    pallas_call x1, Pallas kernels: 12.4 us -> 23.1 us  [sum_blk(): pl.pallas_call(functools.partial(sum_kernel, n), out_shape=jax.ShapeDtype...]
where the time goes in v3:
time: 176 us; the launch traced here: 175 us
  Pallas kernels  146 us (83%)
  local copies, waits for them, and re-layouts  14.9 us (8%)
  other arithmetic  10.7 us (6%)
  matrix products  2.13 us (1%)
  between operations  1.76 us (1%)
    pallas_call x1, Pallas kernels, experts_fused(): pl.pallas_call(functools.partial(experts_kernel, n, g, norm_eps), out_sha...  78.8 us
    pallas_call x3, Pallas kernels, gather_blk(): pl.pallas_call(functools.partial(gather_kernel, n), out_shape=jax.ShapeDt...  35.1 us
    pallas_call x1, Pallas kernels, sum_blk(): pl.pallas_call(functools.partial(sum_kernel, n), out_shape=jax.ShapeDtype...  23.1 us
    unnamed x41, local copies, waits for them, and re-layouts  9.39 us
    pallas_call x1, Pallas kernels, attend_local(): pl.pallas_call(attend_kernel, grid=(KV_HEADS,), out_shape=(jax.ShapeDtype...  9.04 us

profile of v3, /device:TPU:0, one launch (start us, length us, event | category | flops | bytes accessed | tf_op | source)
XLA Modules:
  0.0 175.4 jit_solution(1880486917949856429)
XLA Ops:
  1.8 0.9 copy-done.4
  2.7 13.3 %gather_blk1.1 = bf16[2560,256]{1,0:T(8,128)(2,1)S(1)} custom-call(bf16[320,256]{1,0:T(8,128)(2,1)S(1)} %bitcast.58), custom_call_target="tpu_custom_call" | custom-call | tf_op jit(solution)/shard_map/gather_blk1/pallas_call | solution.py:88
  16.4 0.9 fusion.13.x_ref
  17.3 15.1 %gather_blk2.1 = bf16[3584,256]{1,0:T(8,128)(2,1)S(1)} custom-call(bf16[448,256]{1,0:T(8,128)(2,1)S(1)} %fusion.13.x_ref), custom_call_target="tpu_custom_call" | custom-call | tf_op jit(solution)/shard_map/gather_blk2/pallas_call | solution.py:88
  33.5 0.8 copy-done.7
  35.1 2.8 %gather_fusion = bf16[512,1024]{1,0:T(8,128)(2,1)} fusion(bf16[256,1024]{1,0:T(8,128)(2,1)S(1)} %copy.22, s32[1024]{0:T(1024)S(1)} %pad_clamp_fusion), kind=kCustom, calls=%fused_computation | custom fusion | bytes 2099200 | tf_op jit(solution)/shard_map/gather | solution.py:537
  38.0 1.8 %bitcast_select_fusion.k_ref.v_ref = bf16[512,1024]{1,0:T(8,128)(2,1)S(1)} fusion(bf16[512,1024]{1,0:T(8,128)(2,1)} %gather_fusion, bf16[1,4,128,1024]{3,2,1,0:T(8,128)(2,1)} %param.18, pred[512]{0:T(512)(128)(4,1)S(1)} %fusion.24), kind=kLoop, calls=%fused_computation.20 | loop fusion | flops 524288 | bytes 3146240 | tf_op jit(solution)/shard_map/jit(_where)/select_n | solution.py:538
  39.9 1.2 fusion.3.q_ref
  41.1 0.9 copy.23.kpos_ref
  42.0 1.3 copy-done.1
  43.3 0.9 copy-done.3
  44.3 9.0 %attend_local.1 = (f32[20,128,256]{2,1,0:T(8,128)S(1)}, f32[4,5,256]{2,1,0:T(8,128)S(1)}, f32[4,5,256]{2,1,0:T(8,128)S(1)}) custom-call(bf16[20,128,256]{2,1,0:T(8,128)(2,1)S(1)} %copy-done.1, bf16[512,1024]{1,0:T(8,128)(2,1)S(1)} %bitcast_select_fusion.k_ref.v_ref, bf16[512,1024]{1,0:T(8,128)(2,1)S(1)} %bitcast_select_fusion.k_ref.v_ref, ...), custom_call_target="tpu_custom_call" | custom-call | tf_op jit(solution)/shard_map/attend_local/pallas_call | solution.py:435
  53.3 1.5 copy-done.2
  54.9 6.7 %gather_blk3.1 = f32[320,256]{1,0:T(8,128)S(1)} custom-call(f32[40,256]{1,0:T(8,128)S(1)} %pad_maximum_fusion.1.x_ref), custom_call_target="tpu_custom_call" | custom-call | tf_op jit(solution)/shard_map/gather_blk3/pallas_call | solution.py:88
  61.7 2.0 %multiply_convert_fusion = bf16[20,128,256]{2,1,0:T(8,128)(2,1)S(1)} fusion(f32[20,128,256]{2,1,0:T(8,128)} %copy-done.2, f32[20,256]{1,0:T(8,128)S(1)} %exponential_divide_fusion), kind=kLoop, calls=%fused_computation.6 | loop fusion | flops 1310720 | bytes 3952640 | tf_op jit(solution)/shard_map/convert_element_type | solution.py:551
  63.8 23.1 %sum_blk.1 = bf16[2560,256]{1,0:T(8,128)(2,1)S(1)} custom-call(bf16[2560,256]{1,0:T(8,128)(2,1)S(1)} %bitcast.57), custom_call_target="tpu_custom_call" | custom-call | tf_op jit(solution)/shard_map/sum_blk/pallas_call | solution.py:146
  86.9 1.3 fusion.12.x_ref
  88.2 0.9 copy-done.12
  89.1 2.6 %copy.27 = bf16[320,8,2,384]{3,1,2,0:T(8,128)(2,1)} copy(bf16[320,8,2,384]{3,2,1,0:T(2,128)(2,1)S(1)} %bitcast.62) | data formatting | bytes 7864320
  91.7 1.5 broadcast_in_dim.63.gain_ref
  93.1 0.6 select_reduce_fusion.share_ref
  93.7 78.8 %experts_fused.1 = f32[320,256]{1,0:T(8,128)} custom-call(bf16[320,256]{1,0:T(8,128)(2,1)} %fusion.12.x_ref, f32[2560,1]{1,0:T(8,128)} %broadcast_in_dim.63.gain_ref, f32[8,256]{1,0:T(8,128)} %select_reduce_fusion.share_ref, bf16[2560,768]{1,0:T(8,128)(2,1)} %bitcast.63, bf16[384,2560]{1,0:T(8,128)(2,1)} %bitcast.64, bf16[2560,768]{1,0:T(8,128)(2,1)} %bitcast.59, ...), custom_call_target="tpu_custom_call" | custom-call | tf_op jit(solution)/shard_map/experts_fused/pallas_call | solution.py:372
  172.5 1.7 fusion.19
  174.3 1.1 broadcast_select_fusion
  (61 shorter events, 3.0 us)
Async XLA Ops:
  0.6 15.8 %copy-start = (bf16[2560,448]{0,1:T(8,128)(2,1)S(1)}, bf16[2560,448]{0,1:T(8,128)(2,1)}, u32[]{:S(2)}) copy-start(bf16[2560,448]{0,1:T(8,128)(2,1)} %param.16) | copy-start | bytes 6881284
  0.6 15.8 %copy-start.18 = (f32[2560]{0:T(1024)S(1)}, f32[2560]{0:T(1024)}, u32[]{:S(2)}) copy-start(f32[2560]{0:T(1024)} %param.15) | copy-start | bytes 30724
  1.8 0.9 copy-start.4
  33.5 0.9 copy-start.7
  33.5 1.1 copy-start.9
  33.5 1.4 copy-start.19
  37.9 1.9 %copy-start.8 = (bf16[24,64,256]{2,1,0:T(8,128)(2,1)S(1)}, bf16[24,64,256]{2,1,0:T(8,128)(2,1)}, u32[]{:S(2)}) copy-start(bf16[24,64,256]{2,1,0:T(8,128)(2,1)} %copy-done.7) | copy-start | bytes 2359300
  37.9 2.0 %copy-start.10 = (bf16[24,64,256]{2,1,0:T(8,128)(2,1)S(1)}, bf16[24,64,256]{2,1,0:T(8,128)(2,1)}, u32[]{:S(2)}) copy-start(bf16[24,64,256]{2,1,0:T(8,128)(2,1)} %copy-done.9) | copy-start | bytes 2359300
  42.0 1.3 copy-start.1
  43.3 0.9 copy-start.3
  53.3 1.5 copy-start.2
  63.8 23.1 %copy-start.5 = (bf16[256,320]{0,1:T(8,128)(2,1)S(1)}, bf16[256,320]{0,1:T(8,128)(2,1)}, u32[]{:S(2)}) copy-start(bf16[256,320]{0,1:T(8,128)(2,1)} %param.14) | copy-start | bytes 491524
  63.8 23.1 %copy-start.17 = (bf16[2560,320]{0,1:T(8,128)(2,1)S(1)}, bf16[2560,320]{0,1:T(8,128)(2,1)}, u32[]{:S(2)}) copy-start(bf16[2560,320]{0,1:T(8,128)(2,1)} %param.17) | copy-start | bytes 4915204
  86.9 2.2 %copy-start.12 = (bf16[2560,2,384]{2,1,0:T(2,128)(2,1)S(1)}, bf16[2560,2,384]{2,1,0:T(2,128)(2,1)}, u32[]{:S(2)}) copy-start(bf16[2560,2,384]{2,1,0:T(2,128)(2,1)} %param.24) | copy-start | bytes 11796484
  89.1 2.6 %copy-start.14 = (f32[2560]{0:T(1024)S(1)}, f32[2560]{0:T(1024)}, u32[]{:S(2)}) copy-start(f32[2560]{0:T(1024)} %param.21) | copy-start | bytes 30724
  89.1 4.0 %copy-start.15 = (f32[256,6]{0,1:T(8,128)S(1)}, f32[256,6]{0,1:T(8,128)}, u32[]{:S(2)}) copy-start(f32[256,6]{0,1:T(8,128)} %param.23) | copy-start | bytes 18436
  89.1 4.0 %copy-start.16 = (s32[256,6]{0,1:T(8,128)S(1)}, s32[256,6]{0,1:T(8,128)}, u32[]{:S(2)}) copy-start(s32[256,6]{0,1:T(8,128)} %param.22) | copy-start | bytes 18436
  93.7 78.8 %copy-start.13 = (bf16[320,256]{1,0:T(8,128)(2,1)S(1)}, bf16[320,256]{1,0:T(8,128)(2,1)}, u32[]{:S(2)}) copy-start(bf16[320,256]{1,0:T(8,128)(2,1)} %fusion.12.x_ref) | copy-start | bytes 491524
  93.7 80.5 %copy-start.6 = (bf16[512,1024]{1,0:T(8,128)(2,1)S(1)}, bf16[512,1024]{1,0:T(8,128)(2,1)}, u32[]{:S(2)}) copy-start(bf16[512,1024]{1,0:T(8,128)(2,1)} %gather_fusion) | copy-start | bytes 3145732
  93.7 80.5 %copy-start.11 = (bf16[1,4,128,1024]{3,2,1,0:T(8,128)(2,1)S(1)}, bf16[1,4,128,1024]{3,2,1,0:T(8,128)(2,1)}, u32[]{:S(2)}) copy-start(bf16[1,4,128,1024]{3,2,1,0:T(8,128)(2,1)} %param.18) | copy-start | bytes 3145732

commit v4 on v3

--- a/solution.py
+++ b/solution.py
@@ -332,13 +332,15 @@
     relay(2)
     norm(0)
     hidden_units(sgu, sact, 1.0)
+    turn(3, sdown_raw, sdown, 512)
     for copy in told:
         copy.wait()
+    expert(0)
     arrive(1)
     norm(1)
     expert(1)
     relay(3)
-    turn(3, sdown_raw, sdown, 512)
+    pair(0)
     pair(1)
     arrive(2)
     norm(2)
@@ -348,9 +350,6 @@
     norm(3)
     expert(3)
     pair(3)
-    norm(0)
-    expert(0)
-    pair(0)
     for kz in range(1, g):
         finish(kz)
     total = finish(0)

time: 176 us -> 177 us (level)
  Pallas kernels: 146 us -> 148 us
where the time goes in v4:
time: 177 us
  Pallas kernels  148 us (84%)
  local copies, waits for them, and re-layouts  14.9 us (8%)
  other arithmetic  10.7 us (6%)
  matrix products  2.13 us (1%)
    pallas_call x1, Pallas kernels, experts_fused(): pl.pallas_call(functools.partial(experts_kernel, n, g, norm_eps), out_sha...  80.4 us
    pallas_call x3, Pallas kernels, gather_blk(): pl.pallas_call(functools.partial(gather_kernel, n), out_shape=jax.ShapeDt...  35.1 us
    pallas_call x1, Pallas kernels, sum_blk(): pl.pallas_call(functools.partial(sum_kernel, n), out_shape=jax.ShapeDtype...  23.1 us
    unnamed x41, local copies, waits for them, and re-layouts  9.39 us
    pallas_call x1, Pallas kernels, attend_local(): pl.pallas_call(attend_kernel, grid=(KV_HEADS,), out_shape=(jax.ShapeDtype...  9.04 us

profile of v4, /device:TPU:0, one launch (start us, length us, event | category | flops | bytes accessed | tf_op | source)
XLA Modules:
  0.0 177.1 jit_solution(7318122333343650549)
XLA Ops:
  1.8 0.9 copy-done.4
  2.7 13.3 %gather_blk1.1 = bf16[2560,256]{1,0:T(8,128)(2,1)S(1)} custom-call(bf16[320,256]{1,0:T(8,128)(2,1)S(1)} %bitcast.58), custom_call_target="tpu_custom_call" | custom-call | tf_op jit(solution)/shard_map/gather_blk1/pallas_call | solution.py:88
  16.4 0.9 fusion.13.x_ref
  17.3 15.1 %gather_blk2.1 = bf16[3584,256]{1,0:T(8,128)(2,1)S(1)} custom-call(bf16[448,256]{1,0:T(8,128)(2,1)S(1)} %fusion.13.x_ref), custom_call_target="tpu_custom_call" | custom-call | tf_op jit(solution)/shard_map/gather_blk2/pallas_call | solution.py:88
  33.5 0.8 copy-done.7
  35.1 2.8 %gather_fusion = bf16[512,1024]{1,0:T(8,128)(2,1)} fusion(bf16[256,1024]{1,0:T(8,128)(2,1)S(1)} %copy.22, s32[1024]{0:T(1024)S(1)} %pad_clamp_fusion), kind=kCustom, calls=%fused_computation | custom fusion | bytes 2099200 | tf_op jit(solution)/shard_map/gather | solution.py:536
  38.0 1.8 %bitcast_select_fusion.k_ref.v_ref = bf16[512,1024]{1,0:T(8,128)(2,1)S(1)} fusion(bf16[512,1024]{1,0:T(8,128)(2,1)} %gather_fusion, bf16[1,4,128,1024]{3,2,1,0:T(8,128)(2,1)} %param.18, pred[512]{0:T(512)(128)(4,1)S(1)} %fusion.24), kind=kLoop, calls=%fused_computation.20 | loop fusion | flops 524288 | bytes 3146240 | tf_op jit(solution)/shard_map/jit(_where)/select_n | solution.py:537
  39.9 1.2 fusion.3.q_ref
  41.1 0.9 copy.23.kpos_ref
  42.0 1.3 copy-done.1
  43.3 0.9 copy-done.3
  44.3 9.0 %attend_local.1 = (f32[20,128,256]{2,1,0:T(8,128)S(1)}, f32[4,5,256]{2,1,0:T(8,128)S(1)}, f32[4,5,256]{2,1,0:T(8,128)S(1)}) custom-call(bf16[20,128,256]{2,1,0:T(8,128)(2,1)S(1)} %copy-done.1, bf16[512,1024]{1,0:T(8,128)(2,1)S(1)} %bitcast_select_fusion.k_ref.v_ref, bf16[512,1024]{1,0:T(8,128)(2,1)S(1)} %bitcast_select_fusion.k_ref.v_ref, ...), custom_call_target="tpu_custom_call" | custom-call | tf_op jit(solution)/shard_map/attend_local/pallas_call | solution.py:434
  53.3 1.5 copy-done.2
  54.9 6.7 %gather_blk3.1 = f32[320,256]{1,0:T(8,128)S(1)} custom-call(f32[40,256]{1,0:T(8,128)S(1)} %pad_maximum_fusion.1.x_ref), custom_call_target="tpu_custom_call" | custom-call | tf_op jit(solution)/shard_map/gather_blk3/pallas_call | solution.py:88
  61.7 2.0 %multiply_convert_fusion = bf16[20,128,256]{2,1,0:T(8,128)(2,1)S(1)} fusion(f32[20,128,256]{2,1,0:T(8,128)} %copy-done.2, f32[20,256]{1,0:T(8,128)S(1)} %exponential_divide_fusion), kind=kLoop, calls=%fused_computation.6 | loop fusion | flops 1310720 | bytes 3952640 | tf_op jit(solution)/shard_map/convert_element_type | solution.py:550
  63.8 23.1 %sum_blk.1 = bf16[2560,256]{1,0:T(8,128)(2,1)S(1)} custom-call(bf16[2560,256]{1,0:T(8,128)(2,1)S(1)} %bitcast.57), custom_call_target="tpu_custom_call" | custom-call | tf_op jit(solution)/shard_map/sum_blk/pallas_call | solution.py:146
  86.9 1.3 fusion.12.x_ref
  88.2 0.9 copy-done.12
  89.1 2.6 %copy.27 = bf16[320,8,2,384]{3,1,2,0:T(8,128)(2,1)} copy(bf16[320,8,2,384]{3,2,1,0:T(2,128)(2,1)S(1)} %bitcast.62) | data formatting | bytes 7864320
  91.7 1.5 broadcast_in_dim.63.gain_ref
  93.1 0.6 select_reduce_fusion.share_ref
  93.7 80.4 %experts_fused.1 = f32[320,256]{1,0:T(8,128)} custom-call(bf16[320,256]{1,0:T(8,128)(2,1)} %fusion.12.x_ref, f32[2560,1]{1,0:T(8,128)} %broadcast_in_dim.63.gain_ref, f32[8,256]{1,0:T(8,128)} %select_reduce_fusion.share_ref, bf16[2560,768]{1,0:T(8,128)(2,1)} %bitcast.63, bf16[384,2560]{1,0:T(8,128)(2,1)} %bitcast.64, bf16[2560,768]{1,0:T(8,128)(2,1)} %bitcast.59, ...), custom_call_target="tpu_custom_call" | custom-call | tf_op jit(solution)/shard_map/experts_fused/pallas_call | solution.py:371
  174.2 1.7 fusion.19
  175.9 1.1 broadcast_select_fusion
  (61 shorter events, 3.0 us)
Async XLA Ops:
  0.6 15.8 %copy-start = (bf16[2560,448]{0,1:T(8,128)(2,1)S(1)}, bf16[2560,448]{0,1:T(8,128)(2,1)}, u32[]{:S(2)}) copy-start(bf16[2560,448]{0,1:T(8,128)(2,1)} %param.16) | copy-start | bytes 6881284
  0.6 15.8 %copy-start.18 = (f32[2560]{0:T(1024)S(1)}, f32[2560]{0:T(1024)}, u32[]{:S(2)}) copy-start(f32[2560]{0:T(1024)} %param.15) | copy-start | bytes 30724
  1.8 0.9 copy-start.4
  33.5 0.9 copy-start.7
  33.5 1.1 copy-start.9
  33.5 1.4 copy-start.19
  37.9 1.9 %copy-start.8 = (bf16[24,64,256]{2,1,0:T(8,128)(2,1)S(1)}, bf16[24,64,256]{2,1,0:T(8,128)(2,1)}, u32[]{:S(2)}) copy-start(bf16[24,64,256]{2,1,0:T(8,128)(2,1)} %copy-done.7) | copy-start | bytes 2359300
  37.9 2.0 %copy-start.10 = (bf16[24,64,256]{2,1,0:T(8,128)(2,1)S(1)}, bf16[24,64,256]{2,1,0:T(8,128)(2,1)}, u32[]{:S(2)}) copy-start(bf16[24,64,256]{2,1,0:T(8,128)(2,1)} %copy-done.9) | copy-start | bytes 2359300
  42.0 1.3 copy-start.1
  43.3 0.9 copy-start.3
  53.3 1.5 copy-start.2
  63.8 23.1 %copy-start.5 = (bf16[256,320]{0,1:T(8,128)(2,1)S(1)}, bf16[256,320]{0,1:T(8,128)(2,1)}, u32[]{:S(2)}) copy-start(bf16[256,320]{0,1:T(8,128)(2,1)} %param.14) | copy-start | bytes 491524
  63.8 23.1 %copy-start.17 = (bf16[2560,320]{0,1:T(8,128)(2,1)S(1)}, bf16[2560,320]{0,1:T(8,128)(2,1)}, u32[]{:S(2)}) copy-start(bf16[2560,320]{0,1:T(8,128)(2,1)} %param.17) | copy-start | bytes 4915204
  86.9 2.2 %copy-start.12 = (bf16[2560,2,384]{2,1,0:T(2,128)(2,1)S(1)}, bf16[2560,2,384]{2,1,0:T(2,128)(2,1)}, u32[]{:S(2)}) copy-start(bf16[2560,2,384]{2,1,0:T(2,128)(2,1)} %param.24) | copy-start | bytes 11796484
  89.1 2.6 %copy-start.14 = (f32[2560]{0:T(1024)S(1)}, f32[2560]{0:T(1024)}, u32[]{:S(2)}) copy-start(f32[2560]{0:T(1024)} %param.21) | copy-start | bytes 30724
  89.1 4.0 %copy-start.15 = (f32[256,6]{0,1:T(8,128)S(1)}, f32[256,6]{0,1:T(8,128)}, u32[]{:S(2)}) copy-start(f32[256,6]{0,1:T(8,128)} %param.23) | copy-start | bytes 18436
  89.1 4.0 %copy-start.16 = (s32[256,6]{0,1:T(8,128)S(1)}, s32[256,6]{0,1:T(8,128)}, u32[]{:S(2)}) copy-start(s32[256,6]{0,1:T(8,128)} %param.22) | copy-start | bytes 18436
  93.7 80.4 %copy-start.13 = (bf16[320,256]{1,0:T(8,128)(2,1)S(1)}, bf16[320,256]{1,0:T(8,128)(2,1)}, u32[]{:S(2)}) copy-start(bf16[320,256]{1,0:T(8,128)(2,1)} %fusion.12.x_ref) | copy-start | bytes 491524
  93.7 82.2 %copy-start.6 = (bf16[512,1024]{1,0:T(8,128)(2,1)S(1)}, bf16[512,1024]{1,0:T(8,128)(2,1)}, u32[]{:S(2)}) copy-start(bf16[512,1024]{1,0:T(8,128)(2,1)} %gather_fusion) | copy-start | bytes 3145732
  93.7 82.2 %copy-start.11 = (bf16[1,4,128,1024]{3,2,1,0:T(8,128)(2,1)S(1)}, bf16[1,4,128,1024]{3,2,1,0:T(8,128)(2,1)}, u32[]{:S(2)}) copy-start(bf16[1,4,128,1024]{3,2,1,0:T(8,128)(2,1)} %param.18) | copy-start | bytes 3145732
